TPU v7x, 32 devices: a whole 2x2x4 slice. The times are simulated.
32 devices in a mesh: ctx: 16 (over z, x, core), tp: 2 (over y).
Axes of the slice: x: 2, y: 2, z: 4, core: 2. Of those that a mesh axis runs over, the one named last changes fastest.
Arguments:
- queries: bfloat16 [2048, 4096], P('ctx', 'tp'), may hold values from -6 to 6
- keys: bfloat16 [2048, 8192], P('ctx', 'tp'), may hold values from -6 to 6
- values: bfloat16 [2048, 8192], P('ctx', 'tp'), may hold values from -6 to 6
- beta_logit: float32 [32, 4096], P('tp', 'ctx'), may hold values from -8 to 8
- out_weight: bfloat16 [4096, 4096], P('ctx', 'tp'), may hold values from -0.125 to 0.125
- out_grad: bfloat16 [2048, 4096], P('ctx', 'tp'), may hold values from -6 to 6
Outputs:
- mixed: bfloat16 [2048, 4096], P('ctx', 'tp')
- query_grad: bfloat16 [2048, 4096], P('ctx', 'tp')
- key_grad: bfloat16 [2048, 8192], P('ctx', 'tp')
- value_grad: bfloat16 [2048, 8192], P('ctx', 'tp')
- logit_grad: float32 [32, 4096], P('tp', 'ctx')
- weight_grad: float32 [4096, 4096], P('ctx', 'tp')
All inputs are finite; a program needn't handle non-finite values.
Results may differ from a plain program's by a relative error of at most 0.023.
Values may be sent and summed in bfloat16 or wider, within the bound.
A program may use at most 128 MiB of HBM per device.

v0:
```python
import math

import jax
import jax.numpy as jnp
from jax import lax
from jax.sharding import PartitionSpec as P


def shifted(block, axis, distance):
    devices = range(lax.axis_size(axis))
    route = [(i - distance, i) for i in devices if i - distance in devices]
    return lax.ppermute(block, axis, route)


def normalize(matrix):
    return matrix * lax.rsqrt(jnp.sum(matrix * matrix, axis=-1, keepdims=True) + 1e-06)


def mix_blocks(memory, query_heads, key_heads, value_heads, strength):
    head_count, length, width = query_heads.shape
    blocks = length // 64
    query_blk = query_heads.reshape(head_count, blocks, 64, width).transpose(1, 0, 2, 3)
    key_blk = key_heads.reshape(head_count, blocks, 128, width).transpose(1, 0, 2, 3)
    value_blk = value_heads.reshape(head_count, blocks, 128, value_heads.shape[2]).transpose(
        1, 0, 2, 3
    )
    gate_blk = strength.reshape(head_count, blocks, 128).transpose(1, 0, 2)
    row_ids = lax.broadcasted_iota(jnp.int32, (128, 128), 0)
    col_ids = lax.broadcasted_iota(jnp.int32, (128, 128), 1)
    below_diag = col_ids < row_ids
    token_ids = lax.broadcasted_iota(jnp.int32, (64, 128), 0)
    refl_ids = lax.broadcasted_iota(jnp.int32, (64, 128), 1)
    visible = refl_ids <= 2 * token_ids + 1
    identity_map = jnp.eye(128, dtype=jnp.float32)
    highest = lax.Precision.HIGHEST

    def advance(current, pieces):
        query_x, key_x, value_x, gate_x = pieces
        key_gram = jnp.einsum("hid,hjd->hij", key_x, key_x, precision=highest)
        system = identity_map + jnp.where(below_diag, gate_x[:, :, None] * key_gram, 0.0)
        right_side = gate_x[:, :, None] * (
            value_x - jnp.einsum("hid,hde->hie", key_x, current, precision=highest)
        )
        updates = lax.linalg.triangular_solve(
            system, right_side, left_side=True, lower=True, unit_diagonal=True
        )
        scores = jnp.where(
            visible, jnp.einsum("htd,hid->hti", query_x, key_x, precision=highest), 0.0
        )
        result = jnp.einsum("htd,hde->hte", query_x, current, precision=highest)
        result = result + jnp.einsum("hti,hie->hte", scores, updates, precision=highest)
        current = current + jnp.einsum("hid,hie->hde", key_x, updates, precision=highest)
        return (current, result)

    memory, block_out = lax.scan(advance, memory, (query_blk, key_blk, value_blk, gate_blk))
    block_out = block_out.transpose(1, 0, 2, 3).reshape(head_count, length, block_out.shape[3])
    return (block_out, memory)


def head_layout(query_f, key_f, value_f, logits):
    head_count = logits.shape[0]
    length = query_f.shape[0]
    width = query_f.shape[1] // head_count
    query_heads = normalize(query_f.reshape(length, head_count, width)).transpose(1, 0, 2)
    key_heads = (
        normalize(key_f.reshape(length, head_count, 2, width))
        .transpose(1, 0, 2, 3)
        .reshape(head_count, 2 * length, width)
    )
    value_heads = (
        value_f.reshape(length, head_count, 2, width)
        .transpose(1, 0, 2, 3)
        .reshape(head_count, 2 * length, width)
    )
    strength = 2.0 * jax.nn.sigmoid(logits)
    return (query_heads, key_heads, value_heads, strength)


def group_map(memory, query_f, key_f, value_f, logits):
    head_count = logits.shape[0]
    length = query_f.shape[0]
    width = query_f.shape[1] // head_count
    query_heads, key_heads, value_heads, strength = head_layout(query_f, key_f, value_f, logits)
    block_out, memory = mix_blocks(memory, query_heads, key_heads, value_heads, strength)
    return (block_out.transpose(1, 0, 2).reshape(length, head_count * width), memory)


def matmul_heads(left, right):
    return jnp.einsum("hij,hjk->hik", left, right, precision=lax.Precision.HIGHEST)


def local(queries, keys, values, beta_logit, out_weight, out_grad):
    head_count = beta_logit.shape[0]
    length = queries.shape[0]
    width = queries.shape[1] // head_count
    query_f = queries.astype(jnp.float32)
    key_f = keys.astype(jnp.float32)
    value_f = values.astype(jnp.float32)
    identity_map = jnp.broadcast_to(jnp.eye(width, dtype=jnp.float32), (head_count, width, width))
    zero_state = jnp.zeros((head_count, width, width), jnp.float32)
    query_heads, key_heads, value_heads, strength = head_layout(query_f, key_f, value_f, beta_logit)
    widened_values = jnp.concatenate([jnp.zeros_like(value_heads), value_heads], axis=2)
    widened_start = jnp.concatenate([identity_map, zero_state], axis=2)
    _, widened_end = mix_blocks(widened_start, query_heads, key_heads, widened_values, strength)
    transition = widened_end[:, :, :width]
    offset = widened_end[:, :, width:]

    def hand_on(turn_index, memory):
        return shifted(
            (matmul_heads(transition, memory) + offset).astype(jnp.bfloat16), "ctx", 1
        ).astype(jnp.float32)

    state_in = lax.fori_loop(0, lax.axis_size("ctx") - 1, hand_on, zero_state)
    (heads_f, _), pull = jax.vjp(group_map, state_in, query_f, key_f, value_f, beta_logit)
    heads_out = heads_f.astype(jnp.bfloat16)
    weight_full = lax.all_gather(out_weight, "ctx", axis=0, tiled=True)
    mixed_cols = lax.psum_scatter(
        lax.dot_general(
            weight_full, heads_out, (((1,), (1,)), ((), ())), preferred_element_type=jnp.float32
        ).astype(jnp.bfloat16),
        "tp",
        scatter_dimension=0,
        tiled=True,
    ).astype(jnp.float32)
    mixed = mixed_cols.T.astype(jnp.bfloat16)
    grad_full = lax.all_gather(out_grad, "tp", axis=1, tiled=True)
    head_grad = jnp.dot(grad_full, weight_full, preferred_element_type=jnp.float32)

    def state_only(start_memory):
        return group_map(start_memory, query_f, key_f, value_f, beta_logit)[0]

    _, state_pull = jax.vjp(state_only, state_in)
    own_cotangent = state_pull(head_grad)[0]
    transposed = transition.transpose(0, 2, 1)

    def hand_back(turn_index, memory):
        return shifted(
            (matmul_heads(transposed, memory) + own_cotangent).astype(jnp.bfloat16), "ctx", -1
        ).astype(jnp.float32)

    state_grad = lax.fori_loop(0, lax.axis_size("ctx") - 1, hand_back, zero_state)
    _, query_grad, key_grad, value_grad, logit_grad = pull((head_grad, state_grad))
    scale_factor = 1.0 / math.sqrt(length * lax.axis_size("ctx"))
    product = lax.dot_general(
        grad_full, heads_out, (((0,), (0,)), ((), ())), preferred_element_type=jnp.float32
    )
    weight_grad = lax.psum_scatter(
        (product * scale_factor).astype(jnp.bfloat16), "ctx", scatter_dimension=0, tiled=True
    ).astype(jnp.float32)
    return (
        mixed,
        query_grad.astype(jnp.bfloat16),
        key_grad.astype(jnp.bfloat16),
        value_grad.astype(jnp.bfloat16),
        logit_grad,
        weight_grad,
    )


def solution(mesh):
    placed = (
        P("ctx", "tp"),
        P("ctx", "tp"),
        P("ctx", "tp"),
        P("tp", "ctx"),
        P("ctx", "tp"),
        P("ctx", "tp"),
    )
    return jax.shard_map(
        local,
        mesh=mesh,
        in_specs=placed,
        out_specs=(
            P("ctx", "tp"),
            P("ctx", "tp"),
            P("ctx", "tp"),
            P("ctx", "tp"),
            P("tp", "ctx"),
            P("ctx", "tp"),
        ),
        check_vma=False,
    )
```

profile of v0, /device:TPU:0, one launch (start us, length us, event | category | flops | bytes accessed | tf_op | source)
XLA Modules:
  0.0 2437.0 jit_solution(4699305989843066388)
XLA Ops:
  29.9 356.8 %while.118 = (s32[]{:T(128)}, f32[16,128,256]{2,1,0:T(8,128)}, f32[2,16,128,128]{3,2,1,0:T(8,128)S(1)}, f32[2,16,128]{2,1,0:T(8,128)S(1)}, f32[2,16,128,256]{3,1,2,0:T(8,128)}, /*index=5*/s32[]{:T(128)}) while((s32[]{:T(128)}, f32[16,128,256]{2,1,0:T(8,128)}, f32[2,16,128,128]{3,2,1,0:T(8,128)S(1)}, f32[2,16,128]{2,1,0:T(8,128)S(1)}, ...), condition=%wide.region_2.3_spmd.clone, body=%wide.region_1.2_spmd.clone.sunk | while | flops 2821554176 | bytes 60130484 | solution.py:55
  30.1 5.0 fusion.319
  40.1 158.6 %custom-call.26 = f32[16,1,128,128]{2,3,1,0:T(8,128)} custom-call(f32[16,1,128,128]{3,2,1,0:T(8,128)} %fusion.321), custom_call_target="InvertDiagBlocksLowerTriangular" | custom-call | tf_op jit(solution)/shard_map/while/body/eval_jaxpr/triangular_solve | solution.py:44
  198.7 5.8 fusion.322
  208.4 5.0 fusion.319
  218.4 158.6 %custom-call.26 = f32[16,1,128,128]{2,3,1,0:T(8,128)} custom-call(f32[16,1,128,128]{3,2,1,0:T(8,128)} %fusion.321), custom_call_target="InvertDiagBlocksLowerTriangular" | custom-call | tf_op jit(solution)/shard_map/while/body/eval_jaxpr/triangular_solve | solution.py:44
  377.0 5.8 fusion.322
  408.6 227.6 %while.122 = (s32[]{:T(128)}, f32[16,128,128]{2,1,0:T(8,128)S(1)}, f32[16,128,128]{2,1,0:T(8,128)}, f32[16,128,128]{2,1,0:T(8,128)}, s32[]{:T(128)}, /*index=5*/s32[]{:T(128)}) while((s32[]{:T(128)}, f32[16,128,128]{2,1,0:T(8,128)S(1)}, f32[16,128,128]{2,1,0:T(8,128)}, f32[16,128,128]{2,1,0:T(8,128)}, s32[]{:T(128)}, ...), condition=%wide.region_4.5_spmd.clone, body=%wide.region_3.4_spmd.clone.sunk | while | flops 403701760 | bytes 7340151 | solution.py:113
  421.0 9.8 collective-permute-start
  436.6 9.7 collective-permute-start
  452.1 9.7 collective-permute-start
  467.5 9.7 collective-permute-start
  483.0 9.7 collective-permute-start
  498.5 9.7 collective-permute-start
  513.9 9.7 collective-permute-start
  529.4 9.7 collective-permute-start
  544.9 9.7 collective-permute-start
  560.3 9.7 collective-permute-start
  575.8 9.7 collective-permute-start
  591.3 10.0 collective-permute-start
  607.0 10.6 collective-permute-start
  623.3 10.6 collective-permute-start
  645.2 367.3 %while.119 = (s32[]{:T(128)}, f32[16,128,128]{2,1,0:T(8,128)S(1)}, bf16[2,16,64,128]{3,2,0,1:T(8,128)(2,1)}, f32[2,16,128,128]{3,2,1,0:T(8,128)}, f32[2,16,128,1...) while((s32[]{:T(128)}, f32[16,128,128]{2,1,0:T(8,128)S(1)}, ...), condition=%wide.region_7.8_spmd.clone, body=%wide.region_6.7_spmd.clone.sunk | while | flops 2217820160 | bytes 71766952 | solution.py:55
  658.3 158.6 %custom-call.27 = f32[16,1,128,128]{2,3,1,0:T(8,128)} custom-call(f32[16,1,128,128]{3,2,1,0:T(8,128)} %add_bitcast_fusion.2), custom_call_target="InvertDiagBlocksLowerTriangular" | custom-call | tf_op jit(solution)/shard_map/jvp()/while/body/eval_jaxpr/triangular_solve | solution.py:44
  816.9 4.7 bitcast_dynamic-update-slice_fusion.19
  841.9 158.6 %custom-call.27 = f32[16,1,128,128]{2,3,1,0:T(8,128)} custom-call(f32[16,1,128,128]{3,2,1,0:T(8,128)} %add_bitcast_fusion.2), custom_call_target="InvertDiagBlocksLowerTriangular" | custom-call | tf_op jit(solution)/shard_map/jvp()/while/body/eval_jaxpr/triangular_solve | solution.py:44
  1000.5 4.6 bitcast_dynamic-update-slice_fusion.19
  1013.9 9.5 fusion.195
  1028.1 15.1 while.120
  1043.2 178.7 %reduce-scatter.5.cloned.1.call-done = bf16[256,2048]{0,1:T(8,128)(2,1)} async-done(((bf16[4096,2048]{0,1:T(8,128)(2,1)}), bf16[256,2048]{0,1:T(8,128)(2,1)}) %reduce-scatter.5.cloned.1.call-update) | async-done | bytes 1048592 | tf_op jit(solution)/shard_map/reduce_scatter | solution.py:147
  1224.4 125.5 %all-gather.3.cloned.1.call-done = bf16[4096,2048]{1,0:T(8,128)(2,1)} async-done(((bf16[256,2048]{1,0:T(8,128)(2,1)}), bf16[4096,2048]{1,0:T(8,128)(2,1)}) %all-gather.3.cloned.1.call-update) | async-done | bytes 16777232 | tf_op jit(solution)/shard_map/all_gather | solution.py:116
  1350.0 12.7 fusion.196
  1362.7 8.8 convolution_bitcast_fusion
  1373.0 345.4 %while.123 = (s32[]{:T(128)}, f32[16,128,128]{2,1,0:T(8,128)S(1)}, f32[2,16,64,128]{3,2,1,0:T(8,128)}, f32[2,16,64,128]{3,2,1,0:T(8,128)}, f32[2,16,128,128]{3,2...) while((s32[]{:T(128)}, f32[16,128,128]{2,1,0:T(8,128)S(1)}, ...), condition=%wide.region_12.14_spmd.clone, body=%wide.region_11.13_spmd.clone.sunk | while | flops 1613021312 | bytes 35843816 | solution.py:55
  1373.3 4.0 convolution_add_fusion.35
  1382.7 158.6 %custom-call.29 = f32[16,1,128,128]{2,3,1,0:T(8,128)} custom-call(f32[16,1,128,128]{3,2,1,0:T(8,128)} %fusion.388), custom_call_target="InvertDiagBlocksLowerTriangular" | custom-call | tf_op jit(solution)/shard_map/transpose(jvp())/while/body/eval_jaxpr/triangular_solve/custom-call.2 | solution.py:44
  1545.9 4.0 convolution_add_fusion.35
  1555.3 158.6 %custom-call.29 = f32[16,1,128,128]{2,3,1,0:T(8,128)} custom-call(f32[16,1,128,128]{3,2,1,0:T(8,128)} %fusion.388), custom_call_target="InvertDiagBlocksLowerTriangular" | custom-call | tf_op jit(solution)/shard_map/transpose(jvp())/while/body/eval_jaxpr/triangular_solve/custom-call.2 | solution.py:44
  1718.4 242.6 %while.124 = (s32[]{:T(128)}, f32[16,128,128]{2,1,0:T(8,128)}, f32[16,128,128]{2,1,0:T(8,128)}, f32[16,128,128]{2,1,0:T(8,128)S(1)}, s32[]{:T(128)}, /*index=5*/s32[]{:T(128)}) while((s32[]{:T(128)}, f32[16,128,128]{2,1,0:T(8,128)}, f32[16,128,128]{2,1,0:T(8,128)}, f32[16,128,128]{2,1,0:T(8,128)S(1)}, s32[]{:T(128)}, ...), condition=%wide.region_14.16_spmd.clone, body=%wide.region_13.15_spmd.clone.sunk | while | flops 403701760 | bytes 7340151 | solution.py:141
  1732.7 9.3 collective-permute-done.1
  1749.0 9.5 collective-permute-done.1
  1765.5 9.5 collective-permute-done.1
  1781.9 9.5 collective-permute-done.1
  1798.4 9.5 collective-permute-done.1
  1814.9 9.5 collective-permute-done.1
  1831.4 9.5 collective-permute-done.1
  1847.9 9.5 collective-permute-done.1
  1864.4 9.5 collective-permute-done.1
  1880.8 9.5 collective-permute-done.1
  1897.3 9.5 collective-permute-done.1
  1913.8 10.3 collective-permute-done.1
  1931.0 10.4 collective-permute-done.1
  1948.4 10.4 collective-permute-done.1
  1963.6 453.4 %while.121 = (s32[]{:T(128)}, f32[16,128,128]{2,1,0:T(8,128)}, f32[2,16,64,128]{3,2,0,1:T(8,128)}, f32[2,16,128,128]{3,1,2,0:T(8,128)}, bf16[2,16,128,128]{3,1,2...) while((s32[]{:T(128)}, f32[16,128,128]{2,1,0:T(8,128)}, ...), condition=%wide.region_18.20_spmd.clone, body=%wide.region_15.19_spmd.clone.sunk | while | flops 4838438912 | bytes 142916208 | solution.py:55
  1982.3 4.8 fusion.370
  1987.2 4.5 convolution_add_fusion.29
  1997.9 3.8 convolution_add_fusion.30
  2003.2 157.8 %custom-call.28 = f32[16,1,128,128]{2,3,1,0:T(8,128)} custom-call(f32[16,1,128,128]{3,2,1,0:T(8,128)S(1)} %fusion.366), custom_call_target="InvertDiagBlocksLowerTriangular" | custom-call | tf_op jit(solution)/shard_map/transpose(jvp())/while/body/eval_jaxpr/triangular_solve/custom-call.2 | solution.py:44
  2184.7 4.0 fusion.371
  2199.6 4.8 fusion.370
  2204.4 4.5 convolution_add_fusion.29
  2215.1 3.8 convolution_add_fusion.30
  2220.4 157.8 %custom-call.28 = f32[16,1,128,128]{2,3,1,0:T(8,128)} custom-call(f32[16,1,128,128]{3,2,1,0:T(8,128)S(1)} %fusion.366), custom_call_target="InvertDiagBlocksLowerTriangular" | custom-call | tf_op jit(solution)/shard_map/transpose(jvp())/while/body/eval_jaxpr/triangular_solve/custom-call.2 | solution.py:44
  2402.0 4.0 fusion.371
  (436 shorter events, 451.6 us)
Async XLA Ops:
  7.2 1006.7 %all-gather.5.cloned.1.call-start = ((), (), s32[]{:S(2)}) async-start(), calls=%async_computation.4 | async-start | bytes 1572864 | tf_op jit(solution)/shard_map/all_gather | solution.py:126
  7.9 1214.0 %reduce-scatter.5.cloned.1.call-start = ((), (), s32[]{:S(2)}) async-start(), calls=%async_computation.5 | async-start | bytes 17825792 | tf_op jit(solution)/shard_map/reduce_scatter | solution.py:147
  9.9 4.8 copy-start.41
  9.9 4.7 copy-start.39
  30.1 5.0 copy-start.11
  198.7 5.9 copy-start
  208.4 5.0 copy-start.11
  377.0 5.9 copy-start
  390.0 3.4 copy-start.31
  400.7 7.0 copy-start.45
  400.8 7.0 copy-start.43
  412.1 4.2 collective-permute-start
  421.0 10.9 collective-permute-start
  436.6 10.8 collective-permute-start
  452.1 10.8 collective-permute-start
  467.5 10.8 collective-permute-start
  483.0 10.8 collective-permute-start
  498.5 10.8 collective-permute-start
  513.9 10.8 collective-permute-start
  529.4 10.8 collective-permute-start
  544.9 10.8 collective-permute-start
  560.3 10.8 collective-permute-start
  575.8 10.8 collective-permute-start
  591.3 11.0 collective-permute-start
  607.0 11.7 collective-permute-start
  623.3 11.7 collective-permute-start
  645.2 4.2 copy-start.13
  828.8 4.1 copy-start.13
  1007.1 3.3 copy-start.10
  1007.1 3.3 copy-start.35
  1013.8 9.5 copy-start.30
  1023.4 326.6 %all-gather.3.cloned.1.call-start = ((), (), s32[]{:S(2)}) async-start(), calls=%async_computation.2 | async-start | bytes 17825792 | tf_op jit(solution)/shard_map/all_gather | solution.py:116
  1024.2 1406.1 %reduce-scatter.3.cloned.1.call-start = ((), (), s32[]{:S(2)}) async-start(), calls=%async_computation.3 | async-start | bytes 1572864 | tf_op jit(solution)/shard_map/reduce_scatter | solution.py:117
  1028.1 3.3 copy-start.25
  1035.6 3.3 copy-start.25
  1721.6 4.1 collective-permute-start.1
  1731.4 10.6 collective-permute-start.1
  1747.7 10.8 collective-permute-start.1
  1764.2 10.8 collective-permute-start.1
  1780.7 10.8 collective-permute-start.1
  1797.1 10.8 collective-permute-start.1
  1813.6 10.8 collective-permute-start.1
  1830.1 10.8 collective-permute-start.1
  1846.6 10.8 collective-permute-start.1
  1863.1 10.8 collective-permute-start.1
  1879.5 10.8 collective-permute-start.1
  1896.0 10.8 collective-permute-start.1
  1912.5 11.6 collective-permute-start.1
  1929.7 11.7 collective-permute-start.1
  1947.1 11.7 collective-permute-start.1
  1987.2 4.5 copy-start.18
  2161.0 3.8 copy-start.4
  2167.7 3.4 copy-start.2
  2167.7 6.7 copy-start.33
  2171.1 5.3 copy-start.6
  2184.7 4.0 copy-start.7
  2184.7 4.0 copy-start.8
  2204.4 4.5 copy-start.18
  2378.2 3.8 copy-start.4
  2384.9 3.4 copy-start.2
  2384.9 6.7 copy-start.33
  2388.3 5.3 copy-start.6
  2402.0 4.0 copy-start.7
  2402.0 4.0 copy-start.8
  (48 other events, 94.2 us)
Sparse Core Ops, SparseCore 0:
  9.5 23.9 all-gather.4
  1023.5 198.2 reduce-scatter.4
  1224.0 125.8 all-gather.2
  1362.8 18.4 reduce-scatter.2
where the time goes:
time: 2460 us; the launch traced here: 2440 us
  other arithmetic  1340 us (54%)
  waiting for transfers between devices  460 us (19%)
  matrix products  338 us (14%)
  starting transfers between devices  161 us (7%)
  local copies, waits for them, and re-layouts  102 us (4%)
    another operation x30, other arithmetic, advance(): lax.linalg.triangular_solve(system, right_side, left_side=True, lower=Tru...  1280 us
    reduce_scatter x1, waiting for transfers between devices, local(): lax.psum_scatter((product * scale_factor).astype(jnp.bfloat16), 'ctx', sc...  179 us
    ppermute x30, starting transfers between devices, shifted(): return lax.ppermute(block, axis, route)  161 us
    ppermute x30, waiting for transfers between devices, shifted(): return lax.ppermute(block, axis, route)  155 us
    all_gather x1, waiting for transfers between devices, local(): weight_full = lax.all_gather(out_weight, 'ctx', axis=0, tiled=True)  126 us
    dot_general x30, matrix products, matmul_heads(): jnp.einsum('hij,hjk->hik', left, right, precision=lax.Precision.HIGHEST)  105 us
  transfers between devices with their start and end apart: 34, of which 32 were waited for; matrix products, arithmetic and copies ran while one was open for 72% of the time, Pallas kernels for 0%

commit v1 on v0

v1 whole, which is shorter than its diff:
```python
import functools
import math

import jax
import jax.numpy as jnp
from jax import lax
from jax.experimental import pallas as pl
from jax.experimental.pallas import tpu as pltpu
from jax.sharding import PartitionSpec as P

F32 = jnp.float32
BF16 = jnp.bfloat16
NN = (((1,), (0,)), ((), ()))
NT = (((1,), (1,)), ((), ()))
TN = (((0,), (0,)), ((), ()))
LIMIT = 56 * 1024 * 1024


def halves(x):
    high = x.astype(BF16)
    return (high, (x - high.astype(F32)).astype(BF16))


def mm(left, right, dims=NN):
    total = None
    for i, a in enumerate(left):
        for j, b in enumerate(right):
            if i + j < 2:
                term = lax.dot_general(a, b, dims, preferred_element_type=F32)
                total = term if total is None else total + term
    return total


def inverse_norm(x):
    return lax.rsqrt(jnp.sum(x * x, axis=-1, keepdims=True) + 1e-06)


def stacked(ref, head, width):
    start = head * 2 * width
    return jnp.concatenate(
        [ref[:, start : start + width], ref[:, start + width : start + 2 * width]], axis=0
    )


def time_ids(length, axis):
    ids = lax.broadcasted_iota(jnp.int32, (2 * length, 2 * length), axis)
    second = (ids >= length).astype(jnp.int32)
    return 2 * (ids - second * length) + second


def visible_mask(length):
    token = lax.broadcasted_iota(jnp.int32, (length, 2 * length), 0)
    refl = lax.broadcasted_iota(jnp.int32, (length, 2 * length), 1)
    refl = jnp.where(refl >= length, refl - length, refl)
    return refl <= token


def prepare_kernel(group, q_ref, k_ref, v_ref, b_ref, th_ref, tl_ref, wu_ref, m_ref, off_ref, qe_ref, o0_ref):
    length, width = q_ref.shape[0], q_ref.shape[1] // group
    rows, cols = time_ids(length, 0), time_ids(length, 1)
    visible = visible_mask(length)
    diff = rows ^ cols
    eye = (rows == cols).astype(F32)
    small_eye = (
        lax.broadcasted_iota(jnp.int32, (width, width), 0)
        == lax.broadcasted_iota(jnp.int32, (width, width), 1)
    ).astype(F32)
    state = []
    for g in range(group):
        key = stacked(k_ref, g, width).astype(F32)
        value = stacked(v_ref, g, width).astype(F32)
        query = q_ref[:, g * width : (g + 1) * width].astype(F32)
        key = key * inverse_norm(key)
        query = query * inverse_norm(query)
        b = b_ref[g]
        kp, qp = halves(key), halves(query)
        system = jnp.where(cols < rows, b * mm(kp, kp, NT), 0.0)
        ah, al = halves(system)
        inv = eye - jnp.where(diff == 1, system, 0.0)
        state.append([kp, qp, ah, al, inv, key, query, value, b])
    step = 2
    while step < 2 * length:
        inside = (diff >= step) & (diff < 2 * step)
        for s in state:
            part = (
                jnp.where(inside, s[2], jnp.zeros_like(s[2])),
                jnp.where(inside, s[3], jnp.zeros_like(s[3])),
            )
            ip = halves(s[4])
            s[4] = s[4] - mm(ip, halves(mm(part, ip)))
        step *= 2
    for g, (kp, qp, _, _, inv, key, query, value, b) in enumerate(state):
        ip = halves(inv)
        th_ref[g] = ip[0]
        tl_ref[g] = ip[1]
        wu = mm(ip, halves(b * jnp.concatenate([key, value], axis=1)))
        wu_ref[g] = wu
        wup = halves(wu)
        ku = mm(kp, wup, TN)
        m_hi, m_lo = halves(small_eye - ku[:, :width])
        m_ref[g, 0] = m_hi
        m_ref[g, 1] = m_lo
        off_ref[g] = ku[:, width:]
        scores = jnp.where(visible, mm(qp, kp, NT), 0.0)
        pu = mm(halves(scores), wup)
        q_hi, q_lo = halves(query - pu[:, :width])
        qe_ref[g, 0] = q_hi
        qe_ref[g, 1] = q_lo
        o0_ref[g] = pu[:, width:]


def chain_barrier(me, n):
    barrier = pltpu.get_barrier_semaphore()
    for other in (lax.rem(me + 1, n), lax.rem(me + n - 1, n)):
        pl.semaphore_signal(
            barrier, inc=1, device_id={"ctx": other}, device_id_type=pl.DeviceIdType.MESH
        )
    pl.semaphore_wait(barrier, 2)


def chain(n, place, way, heads, held, out, send_sem, recv_sem, advance):
    me = lax.axis_index("ctx")
    other = lax.rem(me + way + n, n)

    @pl.when(place == 0)
    def _():
        held[...] = jnp.zeros_like(held)

    def move(h):
        return pltpu.make_async_remote_copy(
            src_ref=out.at[h],
            dst_ref=held.at[h],
            send_sem=send_sem.at[h],
            recv_sem=recv_sem.at[h],
            device_id={"ctx": other},
            device_id_type=pl.DeviceIdType.MESH,
        )

    def step(h, carry):
        @pl.when(place > 0)
        def _():
            move(h).wait_recv()

        @pl.when(place < n - 1)
        def _():
            out[h] = advance(h, held[h]).astype(BF16)
            move(h).start()

        return carry

    lax.fori_loop(0, heads, step, 0)

    @pl.when(place < n - 1)
    def _():
        def finish(h, carry):
            move(h).wait_send()
            return carry

        lax.fori_loop(0, heads, finish, 0)


def forward_kernel(n, m_ref, off_ref, qe_ref, o0_ref, s_ref, ho_ref, held, out, send_sem, recv_sem):
    heads, width = off_ref.shape[0], off_ref.shape[1]
    me = lax.axis_index("ctx")
    chain_barrier(me, n)

    def advance(h, state):
        return mm((m_ref[h, 0], m_ref[h, 1]), (state,)) + off_ref[h]

    chain(n, me, 1, heads, held, out, send_sem, recv_sem, advance)
    s_ref[...] = held[...]
    for h in range(heads):
        ho_ref[:, h * width : (h + 1) * width] = (
            mm((qe_ref[h, 0], qe_ref[h, 1]), (held[h],)) + o0_ref[h]
        ).astype(BF16)


def backward_kernel(n, m_ref, qe_ref, do_ref, d_ref, own, held, out, send_sem, recv_sem):
    heads, width = m_ref.shape[0], m_ref.shape[2]
    me = lax.axis_index("ctx")
    chain_barrier(me, n)
    for h in range(heads):
        own[h] = mm(
            (qe_ref[h, 0], qe_ref[h, 1]), halves(do_ref[:, h * width : (h + 1) * width]), TN
        )

    def advance(h, state):
        return mm((m_ref[h, 0], m_ref[h, 1]), (state,), TN) + own[h]

    chain(n, n - 1 - me, -1, heads, held, out, send_sem, recv_sem, advance)
    d_ref[...] = held[...]


def finish_kernel(group, q_ref, k_ref, v_ref, b_ref, th_ref, tl_ref, wu_ref, s_ref, d_ref, do_ref, dq_ref, dk_ref, dv_ref, db_ref):
    length, width = q_ref.shape[0], q_ref.shape[1] // group
    rows, cols = time_ids(length, 0), time_ids(length, 1)
    visible = visible_mask(length)
    below = cols < rows
    for g in range(group):
        here = slice(g * width, (g + 1) * width)
        key = stacked(k_ref, g, width).astype(F32)
        value = stacked(v_ref, g, width).astype(F32)
        query = q_ref[:, here].astype(F32)
        k_norm, q_norm = inverse_norm(key), inverse_norm(query)
        key, query = key * k_norm, query * q_norm
        b = b_ref[g]
        kp, qp = halves(key), halves(query)
        start, end_grad = (s_ref[g],), (d_ref[g],)
        gp = halves(do_ref[:, here])
        gram = mm(kp, kp, NT)
        scores = jnp.where(visible, mm(qp, kp, NT), 0.0)
        wu = wu_ref[g]
        updates = wu[:, width:] - mm(halves(wu[:, :width]), start)
        up = halves(updates)
        update_grad = mm(halves(scores), gp, TN) + mm(kp, end_grad)
        right_grad = mm((th_ref[g], tl_ref[g]), halves(update_grad), TN)
        score_grad = halves(jnp.where(visible, mm(gp, up, NT), 0.0))
        query_grad = mm(gp, start, NT) + mm(score_grad, kp)
        system_grad = jnp.where(below, -mm(halves(right_grad), up, NT), 0.0)
        residual = value - mm(kp, start)
        db_ref[g] = jnp.sum(right_grad * residual, axis=1, keepdims=True) + jnp.sum(
            system_grad * gram, axis=1, keepdims=True
        )
        gram_grad = halves(b * system_grad)
        value_grad = b * right_grad
        key_grad = (
            mm(score_grad, qp, TN)
            + mm(up, end_grad, NT)
            - mm(halves(value_grad), start, NT)
            + mm(gram_grad, kp)
            + mm(gram_grad, kp, TN)
        )
        query_grad = q_norm * (
            query_grad - query * jnp.sum(query * query_grad, axis=1, keepdims=True)
        )
        key_grad = k_norm * (key_grad - key * jnp.sum(key * key_grad, axis=1, keepdims=True))
        dq_ref[:, here] = query_grad.astype(BF16)
        for j in range(2):
            there = slice((2 * g + j) * width, (2 * g + j + 1) * width)
            dk_ref[:, there] = key_grad[j * length : (j + 1) * length].astype(BF16)
            dv_ref[:, there] = value_grad[j * length : (j + 1) * length].astype(BF16)


def per_head(group, *shape):
    return pl.BlockSpec((group,) + shape, lambda i: (i,) + (0,) * len(shape))


def per_column(group, length, width):
    return pl.BlockSpec((length, group * width), lambda i: (0, i))


def local(n, queries, keys, values, beta_logit, out_weight, out_grad):
    heads = beta_logit.shape[0]
    length = queries.shape[0]
    width = queries.shape[1] // heads
    double = 2 * length
    group = 2
    params = pltpu.CompilerParams(vmem_limit_bytes=LIMIT)

    weight_full = lax.all_gather(out_weight, "ctx", axis=0, tiled=True)
    grad_full = lax.all_gather(out_grad, "tp", axis=1, tiled=True)
    grad_cols = lax.all_to_all(grad_full, "ctx", split_axis=1, concat_axis=0, tiled=True)

    strength = 2.0 * jax.nn.sigmoid(beta_logit)
    gate = strength.reshape(heads, length, 2).transpose(0, 2, 1).reshape(heads, double, 1)

    shape = jax.ShapeDtypeStruct
    q_spec, k_spec = per_column(group, length, width), per_column(group, length, 2 * width)
    b_spec = per_head(group, double, 1)
    t_spec = per_head(group, double, double)
    wu_spec = per_head(group, double, 2 * width)
    inv_hi, inv_lo, wu, trans, offset, query_eff, own_out = pl.pallas_call(
        functools.partial(prepare_kernel, group),
        grid=(heads // group,),
        in_specs=[q_spec, k_spec, k_spec, b_spec],
        out_specs=[
            t_spec,
            t_spec,
            wu_spec,
            per_head(group, 2, width, width),
            per_head(group, width, width),
            per_head(group, 2, length, width),
            per_head(group, length, width),
        ],
        out_shape=[
            shape((heads, double, double), BF16),
            shape((heads, double, double), BF16),
            shape((heads, double, 2 * width), F32),
            shape((heads, 2, width, width), BF16),
            shape((heads, width, width), F32),
            shape((heads, 2, length, width), BF16),
            shape((heads, length, width), F32),
        ],
        compiler_params=params,
        name="prepare",
    )(queries, keys, values, gate)

    whole = pl.BlockSpec(memory_space=pltpu.VMEM)
    carried = [
        pltpu.VMEM((heads, width, width), BF16),
        pltpu.VMEM((heads, width, width), BF16),
        pltpu.SemaphoreType.DMA((heads,)),
        pltpu.SemaphoreType.DMA((heads,)),
    ]
    state_in, heads_out = pl.pallas_call(
        functools.partial(forward_kernel, n),
        in_specs=[whole] * 4,
        out_specs=[whole, whole],
        out_shape=[shape((heads, width, width), BF16), shape(queries.shape, BF16)],
        scratch_shapes=carried,
        compiler_params=pltpu.CompilerParams(
            vmem_limit_bytes=LIMIT, collective_id=0, has_side_effects=True
        ),
        name="forward_chain",
    )(trans, offset, query_eff, own_out)

    heads_full = lax.all_gather(heads_out, "ctx", axis=0, tiled=True)
    head_grad = jnp.dot(grad_full, weight_full, preferred_element_type=F32)

    state_grad = pl.pallas_call(
        functools.partial(backward_kernel, n),
        in_specs=[whole] * 3,
        out_specs=whole,
        out_shape=shape((heads, width, width), BF16),
        scratch_shapes=[pltpu.VMEM((heads, width, width), F32)] + carried,
        compiler_params=pltpu.CompilerParams(
            vmem_limit_bytes=LIMIT, collective_id=1, has_side_effects=True
        ),
        name="backward_chain",
    )(trans, query_eff, head_grad)

    mixed_cols = lax.psum_scatter(
        lax.dot_general(weight_full, heads_out, NT, preferred_element_type=F32).astype(BF16),
        "tp",
        scatter_dimension=0,
        tiled=True,
    )
    mixed = mixed_cols.T

    d_spec = per_head(group, width, width)
    query_grad, key_grad, value_grad, gate_grad = pl.pallas_call(
        functools.partial(finish_kernel, group),
        grid=(heads // group,),
        in_specs=[q_spec, k_spec, k_spec, b_spec, t_spec, t_spec, wu_spec, d_spec, d_spec, q_spec],
        out_specs=[q_spec, k_spec, k_spec, b_spec],
        out_shape=[
            shape(queries.shape, BF16),
            shape(keys.shape, BF16),
            shape(values.shape, BF16),
            shape((heads, double, 1), F32),
        ],
        compiler_params=params,
        name="finish",
    )(queries, keys, values, gate, inv_hi, inv_lo, wu, state_in, state_grad, head_grad)

    gate_grad = gate_grad.reshape(heads, 2, length).transpose(0, 2, 1).reshape(heads, double)
    logit_grad = gate_grad * strength * jax.nn.sigmoid(-beta_logit)

    scale_factor = 1.0 / math.sqrt(length * n)
    weight_grad = scale_factor * lax.dot_general(
        grad_cols, heads_full, TN, preferred_element_type=F32
    )
    return (mixed, query_grad, key_grad, value_grad, logit_grad, weight_grad)


def solution(mesh):
    placed = (
        P("ctx", "tp"),
        P("ctx", "tp"),
        P("ctx", "tp"),
        P("tp", "ctx"),
        P("ctx", "tp"),
        P("ctx", "tp"),
    )
    return jax.shard_map(
        functools.partial(local, mesh.shape["ctx"]),
        mesh=mesh,
        in_specs=placed,
        out_specs=(
            P("ctx", "tp"),
            P("ctx", "tp"),
            P("ctx", "tp"),
            P("ctx", "tp"),
            P("tp", "ctx"),
            P("ctx", "tp"),
        ),
        check_vma=False,
    )
```

time: 2460 us -> 360 us (0.15)
  other arithmetic: 1340 us -> 3.57 us
  waiting for transfers between devices: 460 us -> 107 us
  matrix products: 338 us -> 27.9 us
  Pallas kernels: 0 us -> 134 us
  starting transfers between devices: 161 us -> 64.1 us
  local copies, waits for them, and re-layouts: 102 us -> 8.87 us
    another operation x30 -> x0, other arithmetic: 1280 us -> none  [advance(): lax.linalg.triangular_solve(system, right_side, left_side=True, lower=Tru...]
    dot_general x89 -> x3, matrix products: 300 us -> 27.9 us  [the longest x1 12.6 us: local(): lax.dot_general(weight_full, heads_out, NT, preferred_element_type=F32)]
    reduce_scatter x2 -> x1, waiting for transfers between devices: 179 us -> 0.01 us  [local(): lax.psum_scatter(lax.dot_general(weight_full, heads_out, NT, preferred_el...]
    ppermute x30 -> x0, starting transfers between devices: 161 us -> none  [shifted(): return lax.ppermute(block, axis, route)]
    ppermute x30 -> x0, waiting for transfers between devices: 155 us -> none  [shifted(): return lax.ppermute(block, axis, route)]
    pallas_call x0 -> x4, Pallas kernels: none -> 134 us  [the longest x1 53.3 us: local(): pl.pallas_call(functools.partial(prepare_kernel, group), grid=(heads // g...]
    all_gather x1, waiting for transfers between devices: 126 us -> 46 us  [local(): weight_full = lax.all_gather(out_weight, 'ctx', axis=0, tiled=True)]
    all_to_all x0 -> x1, starting transfers between devices: none -> 63.8 us  [local(): lax.all_to_all(grad_full, 'ctx', split_axis=1, concat_axis=0, tiled=True)]
  transfers between devices with their start and end apart: 34 -> 5, of which waited for: 32 -> 2; matrix products, arithmetic and copies ran while one was open for 72% -> 11% of each run, Pallas kernels for 0% -> 37%
where the time goes in v1:
time: 360 us; the launch traced here: 359 us
  Pallas kernels  134 us (37%)
  waiting for transfers between devices  107 us (30%)
  starting transfers between devices  64.1 us (18%)
  matrix products  27.9 us (8%)
  between operations  13.8 us (4%)
  local copies, waits for them, and re-layouts  8.87 us (2%)
    all_to_all x1, starting transfers between devices, local(): lax.all_to_all(grad_full, 'ctx', split_axis=1, concat_axis=0, tiled=True)  63.8 us
    all_gather x1, waiting for transfers between devices, local(): heads_full = lax.all_gather(heads_out, 'ctx', axis=0, tiled=True)  60.4 us
    pallas_call x1, Pallas kernels, local(): pl.pallas_call(functools.partial(prepare_kernel, group), grid=(heads // g...  53.3 us
    all_gather x1, waiting for transfers between devices, local(): weight_full = lax.all_gather(out_weight, 'ctx', axis=0, tiled=True)  46 us
    pallas_call x1, Pallas kernels, local(): pl.pallas_call(functools.partial(backward_kernel, n), in_specs=[whole] *...  40.3 us
    pallas_call x1, Pallas kernels, local(): pl.pallas_call(functools.partial(finish_kernel, group), grid=(heads // gr...  27.5 us
    pallas_call x1, Pallas kernels, local(): pl.pallas_call(functools.partial(forward_kernel, n), in_specs=[whole] * 4...  12.6 us
    dot_general x1, matrix products, local(): lax.dot_general(weight_full, heads_out, NT, preferred_element_type=F32)  12.6 us
  transfers between devices with their start and end apart: 5, of which 2 were waited for; matrix products, arithmetic and copies ran while one was open for 11% of the time, Pallas kernels for 37%

profile of v1, /device:TPU:0, one launch (start us, length us, event | category | flops | bytes accessed | tf_op | source)
XLA Modules:
  0.0 359.2 jit_solution(15955672824808926293)
XLA Ops:
  7.2 0.0 all-gather.6.cloned.1.call-start
  7.2 2.0 copy.40
  9.3 0.0 all-gather.6.cloned.1.call-update
  9.3 0.0 all-gather.4.cloned.1.call-start
  9.3 0.7 all-gather.4.cloned.1.call-update
  10.0 0.0 all-gather.8.cloned.1.call-start
  10.1 0.7 divide_multiply_fusion.1
  10.8 0.1 copy.37
  10.9 0.1 copy.38
  11.0 3.3 reshape.31.b_ref
  14.3 53.3 %prepare.1 = (bf16[16,256,256]{2,1,0:T(8,128)(2,1)}, bf16[16,256,256]{2,1,0:T(8,128)(2,1)}, f32[16,256,256]{2,1,0:T(8,128)}, bf16[16,2,128,128]{3,2,1,0:T(8,128)...) custom-call(bf16[128,2048]{1,0:T(8,128)(2,1)} %q_ref.3, ...), custom_call_target="tpu_custom_call" | custom-call | tf_op jit(solution)/shard_map/prepare/pallas_call | solution.py:272
  67.6 12.6 %forward_chain.1 = (bf16[16,128,128]{2,1,0:T(8,128)(2,1)}, bf16[128,2048]{1,0:T(8,128)(2,1)}) custom-call(bf16[16,2,128,128]{3,2,1,0:T(8,128)(2,1)} %get-tuple-element.19.m_ref, f32[16,128,128]{2,1,0:T(8,128)} %get-tuple-element.20.off_ref, bf16[16,2,128,128]{3,2,1,0:T(8,128)(2,1)} %get-tuple-element.21.qe_ref, f32[16,128,128]{2,1,0:T(8,128)} %get-tuple-element.22.o0_ref), custom_call_target="tpu_custom_call" | custom-call | tf_op jit(solution)/shard_map/forward_chain/pallas_call | solution.py:305
  80.3 0.0 all-gather.8.cloned.1.call-update
  80.3 0.0 all-gather.6.cloned.1.call-done
  80.3 63.8 %all-to-all-start = ((bf16[128,16,256]{0,2,1:T(8,128)(2,1)}), bf16[128,16,256]{0,2,1:T(8,128)(2,1)S(1)}, u32[]{:S(2)}, u32[]{:S(2)}) async-start(bf16[128,16,256]{0,2,1:T(8,128)(2,1)} %bitcast.19), calls=%async_computation.1 | async-start | bytes 2097152 | tf_op jit(solution)/shard_map/all_to_all | solution.py:262
  144.1 0.2 reduce-scatter.2.cloned.1.call-start
  144.3 46.0 %all-gather.4.cloned.1.call-done = bf16[4096,2048]{1,0:T(8,128)(2,1)} async-done(((bf16[256,2048]{1,0:T(8,128)(2,1)}), bf16[4096,2048]{1,0:T(8,128)(2,1)}) %all-gather.4.cloned.1.call-update) | async-done | bytes 16777232 | tf_op jit(solution)/shard_map/all_gather | solution.py:260
  190.3 12.6 %fusion = bf16[4096,128]{0,1:T(8,128)(2,1)} fusion(bf16[128,2048]{1,0:T(8,128)(2,1)} %get-tuple-element.23, bf16[4096,2048]{1,0:T(8,128)(2,1)} %all-gather.4.cloned.1.call-done), kind=kOutput, calls=%fused_computation.1 | convolution fusion | flops 2148007936 | bytes 18350080 | tf_op jit(solution)/shard_map/dot_general | solution.py:333
  202.9 0.0 reduce-scatter.2.cloned.1.call-update
  202.9 0.0 all-to-all-done
  202.9 1.3 copy.44
  204.2 60.4 %all-gather.8.cloned.1.call-done = bf16[2048,2048]{1,0:T(8,128)(2,1)} async-done(((bf16[128,2048]{1,0:T(8,128)(2,1)}), bf16[2048,2048]{1,0:T(8,128)(2,1)}) %all-gather.8.cloned.1.call-update) | async-done | bytes 8388624 | tf_op jit(solution)/shard_map/all_gather | solution.py:317
  264.6 0.0 copy-start
  264.6 6.2 %fusion.1 = f32[256,2048]{0,1:T(8,128)S(1)} fusion(bf16[2048,2048]{1,0:T(8,128)(2,1)} %all-gather.8.cloned.1.call-done, bf16[2048,256]{1,0:T(8,128)(2,1)} %bitcast.21), kind=kOutput, calls=%fused_computation.3 | convolution fusion | flops 2148007936 | bytes 11534336 | tf_op jit(solution)/shard_map/dot_general | solution.py:360
  270.8 1.8 copy.45
  272.6 0.0 copy-done
  272.6 9.1 %fusion.2.do_ref = f32[128,2048]{1,0:T(8,128)} fusion(bf16[128,4096]{0,1:T(8,128)(2,1)S(1)} %copy-done, bf16[4096,2048]{1,0:T(8,128)(2,1)} %all-gather.4.cloned.1.call-done), kind=kOutput, calls=%fused_computation.6 | convolution fusion | flops 2147483648 | bytes 18874368 | tf_op jit(solution)/shard_map/dot_general | solution.py:318
  281.8 40.3 %backward_chain.1.d_ref = bf16[16,128,128]{2,1,0:T(8,128)(2,1)} custom-call(bf16[16,2,128,128]{3,2,1,0:T(8,128)(2,1)} %get-tuple-element.19.m_ref, bf16[16,2,128,128]{3,2,1,0:T(8,128)(2,1)} %get-tuple-element.21.qe_ref, f32[128,2048]{1,0:T(8,128)} %fusion.2.do_ref), custom_call_target="tpu_custom_call" | custom-call | tf_op jit(solution)/shard_map/backward_chain/pallas_call | solution.py:320
  322.1 0.0 copy-start.1
  322.1 27.5 %finish.1 = (bf16[128,2048]{1,0:T(8,128)(2,1)}, bf16[128,4096]{1,0:T(8,128)(2,1)}, bf16[128,4096]{1,0:T(8,128)(2,1)}, f32[16,256,1]{2,1,0:T(8,128)}) custom-call(bf16[128,2048]{1,0:T(8,128)(2,1)} %q_ref.3, bf16[128,4096]{1,0:T(8,128)(2,1)} %k_ref.3, bf16[128,4096]{1,0:T(8,128)(2,1)} %v_ref.3, f32[16,256,1]{2,1,0:T(8,128)} %reshape.31.b_ref, ...), custom_call_target="tpu_custom_call" | custom-call | tf_op jit(solution)/shard_map/finish/pallas_call | solution.py:341
  349.6 2.2 reduce
  351.9 0.1 copy.42
  352.0 0.1 copy.43
  352.1 0.0 copy-done.1
  352.1 0.6 divide_multiply_fusion
  352.7 0.0 reduce-scatter.2.cloned.1.call-done
  (1 shorter events, 0.0 us)
Async XLA Ops:
  7.2 73.1 %all-gather.6.cloned.1.call-start = ((), (), s32[]{:S(2)}) async-start(), calls=%async_computation.4 | async-start | bytes 1572864 | tf_op jit(solution)/shard_map/all_gather | solution.py:261
  9.3 181.0 %all-gather.4.cloned.1.call-start = ((), (), s32[]{:S(2)}) async-start(), calls=%async_computation.2 | async-start | bytes 17825792 | tf_op jit(solution)/shard_map/all_gather | solution.py:260
  10.0 254.6 %all-gather.8.cloned.1.call-start = ((), (), s32[]{:S(2)}) async-start(), calls=%async_computation.5 | async-start | bytes 8912896 | tf_op jit(solution)/shard_map/all_gather | solution.py:317
  80.3 122.6 %all-to-all-start = ((bf16[128,16,256]{0,2,1:T(8,128)(2,1)}), bf16[128,16,256]{0,2,1:T(8,128)(2,1)S(1)}, u32[]{:S(2)}, u32[]{:S(2)}) async-start(bf16[128,16,256]{0,2,1:T(8,128)(2,1)} %bitcast.19), calls=%async_computation.1 | async-start | bytes 2097152 | tf_op jit(solution)/shard_map/all_to_all | solution.py:262
  144.1 208.6 %reduce-scatter.2.cloned.1.call-start = ((), (), s32[]{:S(2)}) async-start(), calls=%async_computation.3 | async-start | bytes 1572864 | tf_op jit(solution)/shard_map/reduce_scatter | solution.py:332
  264.6 8.0 %copy-start = (bf16[128,4096]{0,1:T(8,128)(2,1)S(1)}, bf16[128,4096]{0,1:T(8,128)(2,1)}, u32[]{:S(2)}) copy-start(bf16[128,4096]{0,1:T(8,128)(2,1)} %all-gather.6.cloned.1.call-done) | copy-start | bytes 3145732
  322.1 30.0 %copy-start.1 = (f32[16,256]{1,0:T(8,128)S(1)}, f32[16,256]{1,0:T(8,128)}, u32[]{:S(2)}) copy-start(f32[16,256]{1,0:T(8,128)} %param.9) | copy-start | bytes 49156
Sparse Core Ops, SparseCore 0:
  10.1 24.0 all-gather.5
  36.4 153.8 all-gather.3
  192.5 72.1 all-gather.7
  267.3 18.5 reduce-scatter.1

commit v2 on v1

--- a/solution.py
+++ b/solution.py
@@ -249,6 +249,32 @@
     return pl.BlockSpec((length, group * width), lambda i: (0, i))
 
 
+def both_halves(block):
+    if lax.axis_size("tp") != 2:
+        return lax.all_gather(block, "tp", axis=1, tiled=True)
+    theirs = lax.ppermute(block, "tp", [(0, 1), (1, 0)])
+    first = lax.axis_index("tp") == 0
+    return jnp.concatenate(
+        [jnp.where(first, block, theirs), jnp.where(first, theirs, block)], axis=1
+    )
+
+
+def mixed_share(heads_out, weight_full):
+    size = lax.axis_size("tp")
+    if size != 2:
+        partial = jnp.dot(heads_out, weight_full.T, preferred_element_type=F32).astype(BF16)
+        return lax.psum_scatter(partial, "tp", scatter_dimension=1, tiled=True)
+    half = weight_full.shape[0] // 2
+    me = lax.axis_index("tp")
+
+    def part(index):
+        rows = lax.dynamic_slice_in_dim(weight_full, index * half, half, 0)
+        return lax.dot_general(heads_out, rows, NT, preferred_element_type=F32)
+
+    theirs = lax.ppermute(part(1 - me).astype(BF16), "tp", [(0, 1), (1, 0)])
+    return (part(me) + theirs.astype(F32)).astype(BF16)
+
+
 def local(n, queries, keys, values, beta_logit, out_weight, out_grad):
     heads = beta_logit.shape[0]
     length = queries.shape[0]
@@ -258,7 +284,7 @@
     params = pltpu.CompilerParams(vmem_limit_bytes=LIMIT)
 
     weight_full = lax.all_gather(out_weight, "ctx", axis=0, tiled=True)
-    grad_full = lax.all_gather(out_grad, "tp", axis=1, tiled=True)
+    grad_full = both_halves(out_grad)
     grad_cols = lax.all_to_all(grad_full, "ctx", split_axis=1, concat_axis=0, tiled=True)
 
     strength = 2.0 * jax.nn.sigmoid(beta_logit)
@@ -329,13 +355,8 @@
         name="backward_chain",
     )(trans, query_eff, head_grad)
 
-    mixed_cols = lax.psum_scatter(
-        lax.dot_general(weight_full, heads_out, NT, preferred_element_type=F32).astype(BF16),
-        "tp",
-        scatter_dimension=0,
-        tiled=True,
-    )
-    mixed = mixed_cols.T
+    heads_late, weight_late, _ = lax.optimization_barrier((heads_out, weight_full, state_grad))
+    mixed = mixed_share(heads_late, weight_late)
 
     d_spec = per_head(group, width, width)
     query_grad, key_grad, value_grad, gate_grad = pl.pallas_call(
@@ -356,6 +377,7 @@
     gate_grad = gate_grad.reshape(heads, 2, length).transpose(0, 2, 1).reshape(heads, double)
     logit_grad = gate_grad * strength * jax.nn.sigmoid(-beta_logit)
 
+    heads_full, _ = lax.optimization_barrier((heads_full, query_grad))
     scale_factor = 1.0 / math.sqrt(length * n)
     weight_grad = scale_factor * lax.dot_general(
         grad_cols, heads_full, TN, preferred_element_type=F32

time: 360 us -> 319 us (0.89)
  waiting for transfers between devices: 107 us -> 44.4 us
  Pallas kernels: 134 us -> 146 us
  starting transfers between devices: 64.1 us -> 72.7 us
    all_gather x1, waiting for transfers between devices: 60.4 us -> 0.01 us  [local(): heads_full = lax.all_gather(heads_out, 'ctx', axis=0, tiled=True)]
    all_gather x1, waiting for transfers between devices: 46 us -> 0.02 us  [local(): weight_full = lax.all_gather(out_weight, 'ctx', axis=0, tiled=True)]
    all_to_all x1, waiting for transfers between devices: 0.01 us -> 36 us  [local(): lax.all_to_all(grad_full, 'ctx', split_axis=1, concat_axis=0, tiled=True)]
    pallas_call x1, Pallas kernels: 40.3 us -> 52.6 us  [local(): pl.pallas_call(functools.partial(backward_kernel, n), in_specs=[whole] *...]
    ppermute x0 -> x2, waiting for transfers between devices: none -> 7.66 us  [the longest x1 7.66 us: both_halves(): theirs = lax.ppermute(block, 'tp', [(0, 1), (1, 0)])]
    all_to_all x1, starting transfers between devices: 63.8 us -> 69.5 us  [local(): lax.all_to_all(grad_full, 'ctx', split_axis=1, concat_axis=0, tiled=True)]
    dot_general x1 -> x2, matrix products: 12.6 us -> 13.3 us  [part(): return lax.dot_general(heads_out, rows, NT, preferred_element_type=F32)]
  transfers between devices with their start and end apart: 5 -> 5, of which waited for: 2 -> 2; matrix products, arithmetic and copies ran while one was open for 11% -> 10% of each run, Pallas kernels for 37% -> 46%
where the time goes in v2:
time: 319 us
  Pallas kernels  146 us (46%)
  starting transfers between devices  72.7 us (23%)
  waiting for transfers between devices  44.4 us (14%)
  matrix products  30.4 us (10%)
  between operations  14.2 us (4%)
  local copies, waits for them, and re-layouts  6.41 us (2%)
  other arithmetic  4.68 us (1%)
    all_to_all x1, starting transfers between devices, local(): lax.all_to_all(grad_full, 'ctx', split_axis=1, concat_axis=0, tiled=True)  69.5 us
    pallas_call x1, Pallas kernels, local(): pl.pallas_call(functools.partial(prepare_kernel, group), grid=(heads // g...  53.3 us
    pallas_call x1, Pallas kernels, local(): pl.pallas_call(functools.partial(backward_kernel, n), in_specs=[whole] *...  52.6 us
    all_to_all x1, waiting for transfers between devices, local(): lax.all_to_all(grad_full, 'ctx', split_axis=1, concat_axis=0, tiled=True)  36 us
    pallas_call x1, Pallas kernels, local(): pl.pallas_call(functools.partial(finish_kernel, group), grid=(heads // gr...  27.5 us
    dot_general x2, matrix products, part(): return lax.dot_general(heads_out, rows, NT, preferred_element_type=F32)  13.3 us
    pallas_call x1, Pallas kernels, local(): pl.pallas_call(functools.partial(forward_kernel, n), in_specs=[whole] * 4...  12.7 us
    dot_general x1, matrix products, local(): head_grad = jnp.dot(grad_full, weight_full, preferred_element_type=F32)  10 us
  transfers between devices with their start and end apart: 5, of which 2 were waited for; matrix products, arithmetic and copies ran while one was open for 10% of the time, Pallas kernels for 46%

profile of v2, /device:TPU:0, one launch (start us, length us, event | category | flops | bytes accessed | tf_op | source)
XLA Modules:
  0.0 318.8 jit_solution(14388645198675112820)
XLA Ops:
  7.2 0.0 copy-start.2
  7.2 0.0 all-gather.3.cloned.1.call-start
  7.2 0.7 all-gather.3.cloned.1.call-update
  7.9 0.0 all-gather.5.cloned.1.call-start
  8.0 0.7 divide_multiply_fusion.1
  8.7 0.1 copy.36
  8.8 0.1 copy.37
  8.9 3.3 %reshape.31.b_ref = f32[16,256,1]{2,1,0:T(8,128)} reshape(f32[16,2,128]{2,1,0:T(2,128)S(1)} %copy.37) | data formatting | bytes 32768 | tf_op jit(solution)/shard_map/reshape | solution.py:291
  12.2 53.3 %prepare.1 = (bf16[16,256,256]{2,1,0:T(8,128)(2,1)}, bf16[16,256,256]{2,1,0:T(8,128)(2,1)}, f32[16,256,256]{2,1,0:T(8,128)}, bf16[16,2,128,128]{3,2,1,0:T(8,128)...) custom-call(bf16[128,2048]{1,0:T(8,128)(2,1)} %q_ref.3, ...), custom_call_target="tpu_custom_call" | custom-call | tf_op jit(solution)/shard_map/prepare/pallas_call | solution.py:298
  65.5 12.7 %forward_chain.1 = (bf16[16,128,128]{2,1,0:T(8,128)(2,1)}, bf16[128,2048]{1,0:T(8,128)(2,1)}) custom-call(bf16[16,2,128,128]{3,2,1,0:T(8,128)(2,1)} %get-tuple-element.22.m_ref, f32[16,128,128]{2,1,0:T(8,128)} %get-tuple-element.23.off_ref, bf16[16,2,128,128]{3,2,1,0:T(8,128)(2,1)} %get-tuple-element.24.qe_ref, f32[16,128,128]{2,1,0:T(8,128)} %get-tuple-element.25.o0_ref), custom_call_target="tpu_custom_call" | custom-call | tf_op jit(solution)/shard_map/forward_chain/pallas_call | solution.py:331
  78.2 0.0 all-gather.5.cloned.1.call-update
  78.2 0.0 copy-done.2
  78.2 0.3 copy.40
  78.5 1.6 collective-permute-start
  80.1 7.7 %collective-permute-done = bf16[128,2048]{0,1:T(8,128)(2,1)S(1)} collective-permute-done((bf16[128,2048]{0,1:T(8,128)(2,1)S(1)}, bf16[128,2048]{0,1:T(8,128)(2,1)S(1)}, u32[]{:S(2)}, u32[]{:S(2)}) %collective-permute-start) | collective-permute-done | bytes 524320 | tf_op jit(solution)/shard_map/ppermute | solution.py:255
  87.7 0.1 broadcast_select_fusion.1
  87.8 1.0 pad_maximum_fusion
  88.8 69.5 %all-to-all-start = ((bf16[128,16,256]{0,2,1:T(8,128)(2,1)}), bf16[128,16,256]{0,2,1:T(8,128)(2,1)S(1)}, u32[]{:S(2)}, u32[]{:S(2)}) async-start(bf16[128,16,256]{0,2,1:T(8,128)(2,1)} %bitcast.15), calls=%async_computation | async-start | bytes 2097152 | tf_op jit(solution)/shard_map/all_to_all | solution.py:288
  158.3 36.0 %all-to-all-done = bf16[128,16,256]{0,2,1:T(8,128)(2,1)S(1)} async-done(((bf16[128,16,256]{0,2,1:T(8,128)(2,1)}), bf16[128,16,256]{0,2,1:T(8,128)(2,1)S(1)}, u32[]{:S(2)}, u32[]{:S(2)}) %all-to-all-start) | async-done | bytes 1048608 | tf_op jit(solution)/shard_map/all_to_all | solution.py:288
  194.3 0.0 copy-start.1
  194.3 1.0 copy-done.1
  195.3 1.5 copy.45
  196.8 0.0 copy-start
  196.8 0.0 all-gather.3.cloned.1.call-done
  196.8 10.0 %fusion.11.do_ref = f32[128,2048]{1,0:T(8,128)} fusion(bf16[4096,2048]{1,0:T(8,128)(2,1)} %all-gather.3.cloned.1.call-done, bf16[128,2048]{0,1:T(8,128)(2,1)S(1)} %get-tuple-element.51, bf16[128,2048]{0,1:T(8,128)(2,1)S(1)} %get-tuple-element.50), kind=kOutput, calls=%fused_computation.14 | convolution fusion | flops 2149580800 | bytes 18874368 | tf_op jit(solution)/shard_map/dot_general | solution.py:344
  206.9 52.6 %backward_chain.1.d_ref = bf16[16,128,128]{2,1,0:T(8,128)(2,1)} custom-call(bf16[16,2,128,128]{3,2,1,0:T(8,128)(2,1)} %get-tuple-element.22.m_ref, bf16[16,2,128,128]{3,2,1,0:T(8,128)(2,1)} %get-tuple-element.24.qe_ref, f32[128,2048]{1,0:T(8,128)} %fusion.11.do_ref), custom_call_target="tpu_custom_call" | custom-call | tf_op jit(solution)/shard_map/backward_chain/pallas_call | solution.py:346
  259.5 0.0 copy-done
  259.5 6.3 %fusion.4 = bf16[128,2048]{1,0:T(8,128)(2,1)S(1)} fusion(bf16[128,2048]{1,0:T(8,128)(2,1)S(1)} %copy-done, bf16[4096,2048]{1,0:T(8,128)(2,1)} %all-gather.3.cloned.1.call-done, s32[]{:T(128)S(6)} %select_n.22), kind=kOutput, calls=%fused_computation.5 | convolution fusion | flops 1074003968 | bytes 9437188 | tf_op jit(solution)/shard_map/dot_general | solution.py:272
  265.7 1.6 collective-permute-start.1
  267.3 0.0 copy-start.3
  267.3 27.5 %finish.1 = (bf16[128,2048]{1,0:T(8,128)(2,1)}, bf16[128,4096]{1,0:T(8,128)(2,1)}, bf16[128,4096]{1,0:T(8,128)(2,1)}, f32[16,256,1]{2,1,0:T(8,128)}) custom-call(bf16[128,2048]{1,0:T(8,128)(2,1)} %q_ref.3, bf16[128,4096]{1,0:T(8,128)(2,1)} %k_ref.3, bf16[128,4096]{1,0:T(8,128)(2,1)} %v_ref.3, f32[16,256,1]{2,1,0:T(8,128)} %reshape.31.b_ref, ...), custom_call_target="tpu_custom_call" | custom-call | tf_op jit(solution)/shard_map/finish/pallas_call | solution.py:362
  294.8 2.2 reduce
  297.0 0.1 copy.43
  297.1 0.1 copy.44
  297.2 0.0 copy-done.3
  297.2 0.6 divide_multiply_fusion
  297.9 0.0 all-gather.5.cloned.1.call-done
  297.9 7.0 %convolution_multiply_fusion = f32[256,2048]{1,0:T(8,128)} fusion(bf16[2048,256]{1,0:T(8,128)(2,1)S(1)} %bitcast.13, bf16[2048,2048]{1,0:T(8,128)(2,1)} %all-gather.5.cloned.1.call-done), kind=kOutput, calls=%fused_computation.4 | convolution fusion | flops 2148007936 | bytes 11534336 | tf_op jit(solution)/shard_map/dot_general | solution.py:382
  304.9 0.0 collective-permute-done.1
  304.9 7.1 %add_convert_fusion = bf16[128,2048]{1,0:T(8,128)(2,1)} fusion(bf16[128,2048]{1,0:T(8,128)(2,1)S(1)} %collective-permute-done.1, bf16[128,2048]{1,0:T(8,128)(2,1)S(1)} %copy-done, bf16[4096,2048]{1,0:T(8,128)(2,1)} %all-gather.3.cloned.1.call-done, s32[]{:T(128)S(6)} %select_n.21), kind=kOutput, calls=%fused_computation.7 | convolution fusion | flops 1074528256 | bytes 9961476 | tf_op jit(solution)/shard_map/dot_general | solution.py:272
  (1 shorter events, 0.0 us)
Async XLA Ops:
  7.2 71.0 %copy-start.2 = (bf16[128,2048]{1,0:T(8,128)(2,1)S(1)}, bf16[128,2048]{1,0:T(8,128)(2,1)}, u32[]{:S(2)}) copy-start(bf16[128,2048]{1,0:T(8,128)(2,1)} %param.11) | copy-start | bytes 1572868
  7.2 189.7 %all-gather.3.cloned.1.call-start = ((), (), s32[]{:S(2)}) async-start(), calls=%async_computation.1 | async-start | bytes 17825792 | tf_op jit(solution)/shard_map/all_gather | solution.py:286
  7.9 289.9 %all-gather.5.cloned.1.call-start = ((), (), s32[]{:S(2)}) async-start(), calls=%async_computation.2 | async-start | bytes 8912896 | tf_op jit(solution)/shard_map/all_gather | solution.py:343
  78.5 9.2 %collective-permute-start = (bf16[128,2048]{0,1:T(8,128)(2,1)S(1)}, bf16[128,2048]{0,1:T(8,128)(2,1)S(1)}, u32[]{:S(2)}, u32[]{:S(2)}) collective-permute-start(bf16[128,2048]{0,1:T(8,128)(2,1)S(1)} %copy.40), channel_id=1, source_target_pairs={{0,1},{1,0},{2,3},{3,2},{4,5},{5,4},{6,7},{7,6},{8,9},{9,8},{10,11... | collective-permute-start | bytes 1572872 | tf_op jit(solution)/shard_map/ppermute | solution.py:255
  88.8 105.5 %all-to-all-start = ((bf16[128,16,256]{0,2,1:T(8,128)(2,1)}), bf16[128,16,256]{0,2,1:T(8,128)(2,1)S(1)}, u32[]{:S(2)}, u32[]{:S(2)}) async-start(bf16[128,16,256]{0,2,1:T(8,128)(2,1)} %bitcast.15), calls=%async_computation | async-start | bytes 2097152 | tf_op jit(solution)/shard_map/all_to_all | solution.py:288
  194.3 1.0 copy-start.1
  196.8 62.7 %copy-start = (bf16[128,2048]{1,0:T(8,128)(2,1)S(1)}, bf16[128,2048]{1,0:T(8,128)(2,1)}, u32[]{:S(2)}) copy-start(bf16[128,2048]{1,0:T(8,128)(2,1)} %get-tuple-element.27) | copy-start | bytes 1572868
  265.7 39.2 %collective-permute-start.1 = (bf16[128,2048]{1,0:T(8,128)(2,1)S(1)}, bf16[128,2048]{1,0:T(8,128)(2,1)S(1)}, u32[]{:S(2)}, u32[]{:S(2)}) collective-permute-start(bf16[128,2048]{1,0:T(8,128)(2,1)S(1)} %fusion.4), channel_id=1, source_target_pairs={{0,1},{1,0},{2,3},{3,2},{4,5},{5,4},{6,7},{7,6},{8,9},{9,8},{10,11... | collective-permute-start | bytes 1572872 | tf_op jit(solution)/shard_map/ppermute | solution.py:274
  267.3 29.9 %copy-start.3 = (f32[16,256]{1,0:T(8,128)S(1)}, f32[16,256]{1,0:T(8,128)}, u32[]{:S(2)}) copy-start(f32[16,256]{1,0:T(8,128)} %param.9) | copy-start | bytes 49156
Sparse Core Ops, SparseCore 0:
  10.2 134.2 all-gather.2
  146.7 91.2 all-gather.4

commit v3 on v2

--- a/solution.py
+++ b/solution.py
@@ -53,6 +53,58 @@
     refl = lax.broadcasted_iota(jnp.int32, (length, 2 * length), 1)
     refl = jnp.where(refl >= length, refl - length, refl)
     return refl <= token
+
+
+MESH = pl.DeviceIdType.MESH
+
+
+def greet(devices):
+    barrier = pltpu.get_barrier_semaphore()
+    for device in devices:
+        pl.semaphore_signal(barrier, inc=1, device_id=device, device_id_type=MESH)
+    pl.semaphore_wait(barrier, len(devices))
+
+
+def columns_swap(tp, block, full, sems):
+    me, cols = lax.axis_index("tp"), block.shape[1]
+    sends, receives = [], []
+    for d in range(1, tp):
+        for kept, source in ((sends, me), (receives, lax.rem(me - d + tp, tp))):
+            kept.append(
+                pltpu.make_async_remote_copy(
+                    src_ref=block,
+                    dst_ref=full.at[:, pl.ds(pl.multiple_of(source * cols, 128), cols)],
+                    send_sem=sems[0].at[d - 1],
+                    recv_sem=sems[1].at[d - 1],
+                    device_id={"tp": lax.rem(me + d, tp)},
+                    device_id_type=MESH,
+                )
+            )
+    own = pltpu.make_async_copy(
+        block, full.at[:, pl.ds(pl.multiple_of(me * cols, 128), cols)], sems[2]
+    )
+    return sends, receives, own
+
+
+def swap_prepare_kernel(tp, group, q_ref, k_ref, v_ref, b_ref, g_ref, th_ref, tl_ref, wu_ref, m_ref, off_ref, qe_ref, o0_ref, gf_ref, *sems):
+    step, steps = pl.program_id(0), pl.num_programs(0)
+    sends, receives, own = columns_swap(tp, g_ref, gf_ref, sems)
+
+    @pl.when(step == 0)
+    def _():
+        own.start()
+        greet([{"tp": lax.rem(lax.axis_index("tp") + d, tp)} for d in range(1, tp)])
+        for copy in sends:
+            copy.start()
+
+    prepare_kernel(group, q_ref, k_ref, v_ref, b_ref, th_ref, tl_ref, wu_ref, m_ref, off_ref, qe_ref, o0_ref)
+
+    @pl.when(step == steps - 1)
+    def _():
+        for sent, received in zip(sends, receives):
+            sent.wait_send()
+            received.wait_recv()
+        own.wait()
 
 
 def prepare_kernel(group, q_ref, k_ref, v_ref, b_ref, th_ref, tl_ref, wu_ref, m_ref, off_ref, qe_ref, o0_ref):
@@ -249,16 +301,6 @@
     return pl.BlockSpec((length, group * width), lambda i: (0, i))
 
 
-def both_halves(block):
-    if lax.axis_size("tp") != 2:
-        return lax.all_gather(block, "tp", axis=1, tiled=True)
-    theirs = lax.ppermute(block, "tp", [(0, 1), (1, 0)])
-    first = lax.axis_index("tp") == 0
-    return jnp.concatenate(
-        [jnp.where(first, block, theirs), jnp.where(first, theirs, block)], axis=1
-    )
-
-
 def mixed_share(heads_out, weight_full):
     size = lax.axis_size("tp")
     if size != 2:
@@ -281,12 +323,12 @@
     width = queries.shape[1] // heads
     double = 2 * length
     group = 2
+    tp = lax.axis_size("tp")
+    anywhere = pl.BlockSpec(memory_space=pl.ANY)
+    dma = pltpu.SemaphoreType.DMA
     params = pltpu.CompilerParams(vmem_limit_bytes=LIMIT)
 
     weight_full = lax.all_gather(out_weight, "ctx", axis=0, tiled=True)
-    grad_full = both_halves(out_grad)
-    grad_cols = lax.all_to_all(grad_full, "ctx", split_axis=1, concat_axis=0, tiled=True)
-
     strength = 2.0 * jax.nn.sigmoid(beta_logit)
     gate = strength.reshape(heads, length, 2).transpose(0, 2, 1).reshape(heads, double, 1)
 
@@ -295,10 +337,10 @@
     b_spec = per_head(group, double, 1)
     t_spec = per_head(group, double, double)
     wu_spec = per_head(group, double, 2 * width)
-    inv_hi, inv_lo, wu, trans, offset, query_eff, own_out = pl.pallas_call(
-        functools.partial(prepare_kernel, group),
+    inv_hi, inv_lo, wu, trans, offset, query_eff, own_out, grad_full = pl.pallas_call(
+        functools.partial(swap_prepare_kernel, tp, group),
         grid=(heads // group,),
-        in_specs=[q_spec, k_spec, k_spec, b_spec],
+        in_specs=[q_spec, k_spec, k_spec, b_spec, anywhere],
         out_specs=[
             t_spec,
             t_spec,
@@ -307,6 +349,7 @@
             per_head(group, width, width),
             per_head(group, 2, length, width),
             per_head(group, length, width),
+            anywhere,
         ],
         out_shape=[
             shape((heads, double, double), BF16),
@@ -316,10 +359,16 @@
             shape((heads, width, width), F32),
             shape((heads, 2, length, width), BF16),
             shape((heads, length, width), F32),
+            shape((length, out_grad.shape[1] * tp), BF16),
         ],
-        compiler_params=params,
+        scratch_shapes=[dma((max(tp - 1, 1),)), dma((max(tp - 1, 1),)), dma(())],
+        compiler_params=pltpu.CompilerParams(
+            vmem_limit_bytes=LIMIT, collective_id=2, has_side_effects=True
+        ),
         name="prepare",
-    )(queries, keys, values, gate)
+    )(queries, keys, values, gate, out_grad)
+    grad_cols = lax.all_to_all(grad_full, "ctx", split_axis=1, concat_axis=0, tiled=True)
+    trans, grad_cols = lax.optimization_barrier((trans, grad_cols))
 
     whole = pl.BlockSpec(memory_space=pltpu.VMEM)
     carried = [
@@ -377,7 +426,7 @@
     gate_grad = gate_grad.reshape(heads, 2, length).transpose(0, 2, 1).reshape(heads, double)
     logit_grad = gate_grad * strength * jax.nn.sigmoid(-beta_logit)
 
-    heads_full, _ = lax.optimization_barrier((heads_full, query_grad))
+    heads_full, _, mixed = lax.optimization_barrier((heads_full, query_grad, mixed))
     scale_factor = 1.0 / math.sqrt(length * n)
     weight_grad = scale_factor * lax.dot_general(
         grad_cols, heads_full, TN, preferred_element_type=F32

time: 319 us -> 313 us (0.981)
  starting transfers between devices: 72.7 us -> 2.11 us
  blocking collectives: 0 us -> 53.3 us
  Pallas kernels: 146 us -> 186 us
  waiting for transfers between devices: 44.4 us -> 19.3 us
    all_to_all x1 -> x0, starting transfers between devices: 69.5 us -> none  [local(): lax.all_to_all(grad_full, 'ctx', split_axis=1, concat_axis=0, tiled=True)]
    all_to_all x0 -> x1, blocking collectives: none -> 53.3 us  [local(): lax.all_to_all(grad_full, 'ctx', split_axis=1, concat_axis=0, tiled=True)]
    all_to_all x1 -> x0, waiting for transfers between devices: 36 us -> none  [local(): lax.all_to_all(grad_full, 'ctx', split_axis=1, concat_axis=0, tiled=True)]
    pallas_call x1, Pallas kernels: 52.6 us -> 84.1 us  [local(): pl.pallas_call(functools.partial(backward_kernel, n), in_specs=[whole] *...]
    all_gather x1, waiting for transfers between devices: 0.02 us -> 18.6 us  [local(): weight_full = lax.all_gather(out_weight, 'ctx', axis=0, tiled=True)]
    ppermute x1 -> x0, waiting for transfers between devices: 7.66 us -> none  [both_halves(): theirs = lax.ppermute(block, 'tp', [(0, 1), (1, 0)])]
    pallas_call x1, Pallas kernels: 12.7 us -> 17.1 us  [local(): pl.pallas_call(functools.partial(forward_kernel, n), in_specs=[whole] * 4...]
    pallas_call x1, Pallas kernels: 53.3 us -> 57 us  [local(): pl.pallas_call(functools.partial(swap_prepare_kernel, tp, group), grid=(h...]
  transfers between devices with their start and end apart: 5 -> 3, of which waited for: 2 -> 1; matrix products, arithmetic and copies ran while one was open for 10% -> 10% of each run, Pallas kernels for 46% -> 59%
where the time goes in v3:
time: 313 us
  Pallas kernels  186 us (59%)
  blocking collectives  53.3 us (17%)
  matrix products  29.6 us (9%)
  waiting for transfers between devices  19.3 us (6%)
  between operations  14.1 us (5%)
  local copies, waits for them, and re-layouts  5.1 us (2%)
  other arithmetic  3.57 us (1%)
    pallas_call x1, Pallas kernels, local(): pl.pallas_call(functools.partial(backward_kernel, n), in_specs=[whole] *...  84.1 us
    pallas_call x1, Pallas kernels, local(): pl.pallas_call(functools.partial(swap_prepare_kernel, tp, group), grid=(h...  57 us
    all_to_all x1, blocking collectives, local(): lax.all_to_all(grad_full, 'ctx', split_axis=1, concat_axis=0, tiled=True)  53.3 us
    pallas_call x1, Pallas kernels, local(): pl.pallas_call(functools.partial(finish_kernel, group), grid=(heads // gr...  27.5 us
    all_gather x1, waiting for transfers between devices, local(): weight_full = lax.all_gather(out_weight, 'ctx', axis=0, tiled=True)  18.6 us
    pallas_call x1, Pallas kernels, local(): pl.pallas_call(functools.partial(forward_kernel, n), in_specs=[whole] * 4...  17.1 us
    dot_general x2, matrix products, part(): return lax.dot_general(heads_out, rows, NT, preferred_element_type=F32)  13.5 us
    dot_general x1, matrix products, local(): head_grad = jnp.dot(grad_full, weight_full, preferred_element_type=F32)  9.07 us
  transfers between devices with their start and end apart: 3, of which 1 were waited for; matrix products, arithmetic and copies ran while one was open for 10% of the time, Pallas kernels for 59%

profile of v3, /device:TPU:0, one launch (start us, length us, event | category | flops | bytes accessed | tf_op | source)
XLA Modules:
  0.0 312.7 jit_solution(2982291552869138278)
XLA Ops:
  7.2 0.0 all-gather.5.cloned.1.call-start
  7.2 0.7 all-gather.5.cloned.1.call-update
  7.9 0.0 all-gather.3.cloned.1.call-start
  7.9 0.7 divide_multiply_fusion.1
  8.7 0.1 copy.24
  8.8 0.1 copy.25
  8.8 3.3 %reshape.31.b_ref = f32[16,256,1]{2,1,0:T(8,128)} reshape(f32[16,2,128]{2,1,0:T(2,128)S(1)} %copy.25) | data formatting | bytes 32768 | tf_op jit(solution)/shard_map/reshape | solution.py:333
  12.2 57.0 %prepare.1 = (bf16[16,256,256]{2,1,0:T(8,128)(2,1)}, bf16[16,256,256]{2,1,0:T(8,128)(2,1)}, f32[16,256,256]{2,1,0:T(8,128)}, bf16[16,2,128,128]{3,2,1,0:T(8,128)...) custom-call(bf16[128,2048]{1,0:T(8,128)(2,1)} %q_ref.3, ...), custom_call_target="tpu_custom_call" | custom-call | tf_op jit(solution)/shard_map/prepare/pallas_call | solution.py:340
  69.2 0.0 copy-start
  69.2 1.4 copy.33
  70.6 53.3 %all_to_all.19 = bf16[128,16,256]{2,0,1:T(8,128)(2,1)S(1)} all-to-all(bf16[128,16,256]{2,0,1:T(8,128)(2,1)S(1)} %bitcast.20), channel_id=1, replica_groups=mesh['ctx'=16,'tp'=2] {'ctx'}, dimensions={1} | all-to-all | bytes 2097152 | tf_op jit(solution)/shard_map/all_to_all | solution.py:370
  123.9 17.1 %forward_chain.1 = (bf16[16,128,128]{2,1,0:T(8,128)(2,1)}, bf16[128,2048]{1,0:T(8,128)(2,1)}) custom-call(bf16[16,2,128,128]{3,2,1,0:T(8,128)(2,1)} %get-tuple-element.28.m_ref, f32[16,128,128]{2,1,0:T(8,128)} %get-tuple-element.29.off_ref, bf16[16,2,128,128]{3,2,1,0:T(8,128)(2,1)} %get-tuple-element.30.qe_ref, f32[16,128,128]{2,1,0:T(8,128)} %get-tuple-element.31.o0_ref), custom_call_target="tpu_custom_call" | custom-call | tf_op jit(solution)/shard_map/forward_chain/pallas_call | solution.py:380
  141.0 0.0 all-gather.3.cloned.1.call-update
  141.0 0.0 copy-start.1
  141.0 18.6 %all-gather.5.cloned.1.call-done = bf16[4096,2048]{1,0:T(8,128)(2,1)} async-done(((bf16[256,2048]{1,0:T(8,128)(2,1)}), bf16[4096,2048]{1,0:T(8,128)(2,1)}) %all-gather.5.cloned.1.call-update) | async-done | bytes 16777232 | tf_op jit(solution)/shard_map/all_gather | solution.py:331
  159.6 0.0 copy-done
  159.6 9.1 %fusion.11.do_ref = f32[128,2048]{1,0:T(8,128)} fusion(bf16[128,4096]{1,0:T(8,128)(2,1)S(1)} %copy-done, bf16[4096,2048]{1,0:T(8,128)(2,1)} %all-gather.5.cloned.1.call-done), kind=kOutput, calls=%fused_computation.12 | convolution fusion | flops 2147483648 | bytes 18874368 | tf_op jit(solution)/shard_map/dot_general | solution.py:393
  168.7 84.1 %backward_chain.1.d_ref = bf16[16,128,128]{2,1,0:T(8,128)(2,1)} custom-call(bf16[16,2,128,128]{3,2,1,0:T(8,128)(2,1)} %get-tuple-element.28.m_ref, bf16[16,2,128,128]{3,2,1,0:T(8,128)(2,1)} %get-tuple-element.30.qe_ref, f32[128,2048]{1,0:T(8,128)} %fusion.11.do_ref), custom_call_target="tpu_custom_call" | custom-call | tf_op jit(solution)/shard_map/backward_chain/pallas_call | solution.py:395
  252.8 0.0 copy-done.1
  252.8 6.4 %fusion.4 = bf16[128,2048]{1,0:T(8,128)(2,1)S(1)} fusion(bf16[128,2048]{1,0:T(8,128)(2,1)S(1)} %copy-done.1, bf16[4096,2048]{1,0:T(8,128)(2,1)} %all-gather.5.cloned.1.call-done, s32[]{:T(128)S(6)} %select_n.7), kind=kOutput, calls=%fused_computation.5 | convolution fusion | flops 1074003968 | bytes 9437188 | tf_op jit(solution)/shard_map/dot_general | solution.py:314
  259.2 2.0 collective-permute-start
  261.2 0.0 copy-start.2
  261.2 27.5 %finish.1 = (bf16[128,2048]{1,0:T(8,128)(2,1)}, bf16[128,4096]{1,0:T(8,128)(2,1)}, bf16[128,4096]{1,0:T(8,128)(2,1)}, f32[16,256,1]{2,1,0:T(8,128)}) custom-call(bf16[128,2048]{1,0:T(8,128)(2,1)} %q_ref.3, bf16[128,4096]{1,0:T(8,128)(2,1)} %k_ref.3, bf16[128,4096]{1,0:T(8,128)(2,1)} %v_ref.3, f32[16,256,1]{2,1,0:T(8,128)} %reshape.31.b_ref, ...), custom_call_target="tpu_custom_call" | custom-call | tf_op jit(solution)/shard_map/finish/pallas_call | solution.py:411
  288.7 2.2 reduce
  290.9 0.1 copy.29
  291.1 0.1 copy.30
  291.1 0.0 copy-done.2
  291.1 0.6 divide_multiply_fusion
  291.8 0.0 collective-permute-done
  291.8 7.1 %add_convert_fusion = bf16[128,2048]{1,0:T(8,128)(2,1)} fusion(bf16[128,2048]{1,0:T(8,128)(2,1)S(1)} %collective-permute-done, bf16[128,2048]{1,0:T(8,128)(2,1)S(1)} %copy-done.1, bf16[4096,2048]{1,0:T(8,128)(2,1)} %all-gather.5.cloned.1.call-done, s32[]{:T(128)S(6)} %select_n.6), kind=kOutput, calls=%fused_computation.7 | convolution fusion | flops 1074528256 | bytes 9961476 | tf_op jit(solution)/shard_map/dot_general | solution.py:314
  298.8 0.0 all-gather.3.cloned.1.call-done
  298.8 7.0 %convolution_multiply_fusion = f32[256,2048]{1,0:T(8,128)} fusion(bf16[2048,256]{1,0:T(8,128)(2,1)S(1)} %bitcast.18, bf16[2048,2048]{1,0:T(8,128)(2,1)} %all-gather.3.cloned.1.call-done), kind=kOutput, calls=%fused_computation.4 | convolution fusion | flops 2148007936 | bytes 11534336 | tf_op jit(solution)/shard_map/dot_general | solution.py:431
  (1 shorter events, 0.0 us)
Async XLA Ops:
  7.2 152.4 %all-gather.5.cloned.1.call-start = ((), (), s32[]{:S(2)}) async-start(), calls=%async_computation.2 | async-start | bytes 17825792 | tf_op jit(solution)/shard_map/all_gather | solution.py:331
  7.9 290.9 %all-gather.3.cloned.1.call-start = ((), (), s32[]{:S(2)}) async-start(), calls=%async_computation.1 | async-start | bytes 8912896 | tf_op jit(solution)/shard_map/all_gather | solution.py:392
  69.2 90.5 %copy-start = (bf16[128,4096]{1,0:T(8,128)(2,1)S(1)}, bf16[128,4096]{1,0:T(8,128)(2,1)}, u32[]{:S(2)}) copy-start(bf16[128,4096]{1,0:T(8,128)(2,1)} %get-tuple-element.27) | copy-start | bytes 3145732
  141.0 111.8 %copy-start.1 = (bf16[128,2048]{1,0:T(8,128)(2,1)S(1)}, bf16[128,2048]{1,0:T(8,128)(2,1)}, u32[]{:S(2)}) copy-start(bf16[128,2048]{1,0:T(8,128)(2,1)} %get-tuple-element.38) | copy-start | bytes 1572868
  259.2 32.6 %collective-permute-start = (bf16[128,2048]{1,0:T(8,128)(2,1)S(1)}, bf16[128,2048]{1,0:T(8,128)(2,1)S(1)}, u32[]{:S(2)}, u32[]{:S(2)}) collective-permute-start(bf16[128,2048]{1,0:T(8,128)(2,1)S(1)} %fusion.4), channel_id=1, source_target_pairs={{0,1},{1,0},{2,3},{3,2},{4,5},{5,4},{6,7},{7,6},{8,9},{9,8},{10,11... | collective-permute-start | bytes 1572872 | tf_op jit(solution)/shard_map/ppermute | solution.py:316
  261.2 29.9 %copy-start.2 = (f32[16,256]{1,0:T(8,128)S(1)}, f32[16,256]{1,0:T(8,128)}, u32[]{:S(2)}) copy-start(f32[16,256]{1,0:T(8,128)} %param.9) | copy-start | bytes 49156
Sparse Core Ops, SparseCore 0:
  10.2 149.3 all-gather.4
  161.8 96.4 all-gather.2

commit v4 on v3

--- a/solution.py
+++ b/solution.py
@@ -389,7 +389,6 @@
         name="forward_chain",
     )(trans, offset, query_eff, own_out)
 
-    heads_full = lax.all_gather(heads_out, "ctx", axis=0, tiled=True)
     head_grad = jnp.dot(grad_full, weight_full, preferred_element_type=F32)
 
     state_grad = pl.pallas_call(
@@ -404,7 +403,10 @@
         name="backward_chain",
     )(trans, query_eff, head_grad)
 
-    heads_late, weight_late, _ = lax.optimization_barrier((heads_out, weight_full, state_grad))
+    heads_late, weight_late, state_grad = lax.optimization_barrier(
+        (heads_out, weight_full, state_grad)
+    )
+    heads_full = lax.all_gather(heads_late, "ctx", axis=0, tiled=True)
     mixed = mixed_share(heads_late, weight_late)
 
     d_spec = per_head(group, width, width)

time: 313 us -> 313 us (level)
  Pallas kernels: 186 us -> 159 us
  waiting for transfers between devices: 19.3 us -> 46.1 us
    all_gather x1, waiting for transfers between devices: 0.01 us -> 26.8 us  [local(): heads_full = lax.all_gather(heads_late, 'ctx', axis=0, tiled=True)]
    pallas_call x1, Pallas kernels: 84.1 us -> 58 us  [local(): pl.pallas_call(functools.partial(backward_kernel, n), in_specs=[whole] *...]
  transfers between devices with their start and end apart: 3 -> 3, of which waited for: 1 -> 2; matrix products, arithmetic and copies ran while one was open for 10% -> 7% of each run, Pallas kernels for 59% -> 32%
where the time goes in v4:
time: 313 us
  Pallas kernels  159 us (51%)
  blocking collectives  53.3 us (17%)
  waiting for transfers between devices  46.1 us (15%)
  matrix products  29.5 us (9%)
  between operations  14.1 us (5%)
  local copies, waits for them, and re-layouts  5.1 us (2%)
  other arithmetic  3.57 us (1%)
    pallas_call x1, Pallas kernels, local(): pl.pallas_call(functools.partial(backward_kernel, n), in_specs=[whole] *...  58 us
    pallas_call x1, Pallas kernels, local(): pl.pallas_call(functools.partial(swap_prepare_kernel, tp, group), grid=(h...  57 us
    all_to_all x1, blocking collectives, local(): lax.all_to_all(grad_full, 'ctx', split_axis=1, concat_axis=0, tiled=True)  53.3 us
    pallas_call x1, Pallas kernels, local(): pl.pallas_call(functools.partial(finish_kernel, group), grid=(heads // gr...  27.5 us
    all_gather x1, waiting for transfers between devices, local(): heads_full = lax.all_gather(heads_late, 'ctx', axis=0, tiled=True)  26.8 us
    all_gather x1, waiting for transfers between devices, local(): weight_full = lax.all_gather(out_weight, 'ctx', axis=0, tiled=True)  18.6 us
    pallas_call x1, Pallas kernels, local(): pl.pallas_call(functools.partial(forward_kernel, n), in_specs=[whole] * 4...  17.1 us
    dot_general x2, matrix products, part(): return lax.dot_general(heads_out, rows, NT, preferred_element_type=F32)  13.4 us
  transfers between devices with their start and end apart: 3, of which 2 were waited for; matrix products, arithmetic and copies ran while one was open for 7% of the time, Pallas kernels for 32%

profile of v4, /device:TPU:0, one launch (start us, length us, event | category | flops | bytes accessed | tf_op | source)
XLA Modules:
  0.0 312.8 jit_solution(18017455846527807348)
XLA Ops:
  7.2 0.0 all-gather.3.cloned.1.call-start
  7.2 0.7 all-gather.3.cloned.1.call-update
  7.9 0.0 all-gather.5.cloned.1.call-start
  7.9 0.7 divide_multiply_fusion.1
  8.7 0.1 copy.24
  8.8 0.1 copy.25
  8.8 3.3 %reshape.31.b_ref = f32[16,256,1]{2,1,0:T(8,128)} reshape(f32[16,2,128]{2,1,0:T(2,128)S(1)} %copy.25) | data formatting | bytes 32768 | tf_op jit(solution)/shard_map/reshape | solution.py:333
  12.2 57.0 %prepare.1 = (bf16[16,256,256]{2,1,0:T(8,128)(2,1)}, bf16[16,256,256]{2,1,0:T(8,128)(2,1)}, f32[16,256,256]{2,1,0:T(8,128)}, bf16[16,2,128,128]{3,2,1,0:T(8,128)...) custom-call(bf16[128,2048]{1,0:T(8,128)(2,1)} %q_ref.3, ...), custom_call_target="tpu_custom_call" | custom-call | tf_op jit(solution)/shard_map/prepare/pallas_call | solution.py:340
  69.1 0.0 copy-start
  69.1 1.4 copy.33
  70.6 53.3 %all_to_all.19 = bf16[128,16,256]{2,0,1:T(8,128)(2,1)S(1)} all-to-all(bf16[128,16,256]{2,0,1:T(8,128)(2,1)S(1)} %bitcast.20), channel_id=1, replica_groups=mesh['ctx'=16,'tp'=2] {'ctx'}, dimensions={1} | all-to-all | bytes 2097152 | tf_op jit(solution)/shard_map/all_to_all | solution.py:370
  123.9 17.1 %forward_chain.1 = (bf16[16,128,128]{2,1,0:T(8,128)(2,1)}, bf16[128,2048]{1,0:T(8,128)(2,1)}) custom-call(bf16[16,2,128,128]{3,2,1,0:T(8,128)(2,1)} %get-tuple-element.29.m_ref, f32[16,128,128]{2,1,0:T(8,128)} %get-tuple-element.30.off_ref, bf16[16,2,128,128]{3,2,1,0:T(8,128)(2,1)} %get-tuple-element.31.qe_ref, f32[16,128,128]{2,1,0:T(8,128)} %get-tuple-element.32.o0_ref), custom_call_target="tpu_custom_call" | custom-call | tf_op jit(solution)/shard_map/forward_chain/pallas_call | solution.py:380
  141.0 0.0 copy-start.1
  141.0 18.6 %all-gather.3.cloned.1.call-done = bf16[4096,2048]{1,0:T(8,128)(2,1)} async-done(((bf16[256,2048]{1,0:T(8,128)(2,1)}), bf16[4096,2048]{1,0:T(8,128)(2,1)}) %all-gather.3.cloned.1.call-update) | async-done | bytes 16777232 | tf_op jit(solution)/shard_map/all_gather | solution.py:331
  159.6 0.0 copy-done
  159.6 9.1 %fusion.11.do_ref = f32[128,2048]{1,0:T(8,128)} fusion(bf16[128,4096]{1,0:T(8,128)(2,1)S(1)} %copy-done, bf16[4096,2048]{1,0:T(8,128)(2,1)} %all-gather.3.cloned.1.call-done), kind=kOutput, calls=%fused_computation.12 | convolution fusion | flops 2147483648 | bytes 18874368 | tf_op jit(solution)/shard_map/dot_general | solution.py:392
  168.7 58.0 %backward_chain.1.d_ref = bf16[16,128,128]{2,1,0:T(8,128)(2,1)} custom-call(bf16[16,2,128,128]{3,2,1,0:T(8,128)(2,1)} %get-tuple-element.29.m_ref, bf16[16,2,128,128]{3,2,1,0:T(8,128)(2,1)} %get-tuple-element.31.qe_ref, f32[128,2048]{1,0:T(8,128)} %fusion.11.do_ref), custom_call_target="tpu_custom_call" | custom-call | tf_op jit(solution)/shard_map/backward_chain/pallas_call | solution.py:394
  226.7 0.0 all-gather.5.cloned.1.call-update
  226.7 0.0 copy-done.1
  226.7 6.3 %fusion.4 = bf16[128,2048]{1,0:T(8,128)(2,1)S(1)} fusion(bf16[128,2048]{1,0:T(8,128)(2,1)S(1)} %copy-done.1, bf16[4096,2048]{1,0:T(8,128)(2,1)} %all-gather.3.cloned.1.call-done, s32[]{:T(128)S(6)} %select_n.7), kind=kOutput, calls=%fused_computation.5 | convolution fusion | flops 1074003968 | bytes 9437188 | tf_op jit(solution)/shard_map/dot_general | solution.py:314
  233.0 1.5 collective-permute-start
  234.5 0.0 copy-start.2
  234.5 27.5 %finish.1 = (bf16[128,2048]{1,0:T(8,128)(2,1)}, bf16[128,4096]{1,0:T(8,128)(2,1)}, bf16[128,4096]{1,0:T(8,128)(2,1)}, f32[16,256,1]{2,1,0:T(8,128)}) custom-call(bf16[128,2048]{1,0:T(8,128)(2,1)} %q_ref.3, bf16[128,4096]{1,0:T(8,128)(2,1)} %k_ref.3, bf16[128,4096]{1,0:T(8,128)(2,1)} %v_ref.3, f32[16,256,1]{2,1,0:T(8,128)} %reshape.31.b_ref, ...), custom_call_target="tpu_custom_call" | custom-call | tf_op jit(solution)/shard_map/finish/pallas_call | solution.py:413
  261.9 2.2 reduce
  264.2 0.1 copy.29
  264.3 0.1 copy.30
  264.3 0.0 copy-done.2
  264.3 0.6 divide_multiply_fusion
  265.0 0.0 collective-permute-done
  265.0 7.1 %add_convert_fusion = bf16[128,2048]{1,0:T(8,128)(2,1)} fusion(bf16[128,2048]{1,0:T(8,128)(2,1)S(1)} %collective-permute-done, bf16[128,2048]{1,0:T(8,128)(2,1)S(1)} %copy-done.1, bf16[4096,2048]{1,0:T(8,128)(2,1)} %all-gather.3.cloned.1.call-done, s32[]{:T(128)S(6)} %select_n.6), kind=kOutput, calls=%fused_computation.7 | convolution fusion | flops 1074528256 | bytes 9961476 | tf_op jit(solution)/shard_map/dot_general | solution.py:314
  272.1 26.8 %all-gather.5.cloned.1.call-done = bf16[2048,2048]{1,0:T(8,128)(2,1)} async-done(((bf16[128,2048]{1,0:T(8,128)(2,1)}), bf16[2048,2048]{1,0:T(8,128)(2,1)}) %all-gather.5.cloned.1.call-update) | async-done | bytes 8388624 | tf_op jit(solution)/shard_map/all_gather | solution.py:409
  298.9 7.0 %convolution_multiply_fusion = f32[256,2048]{1,0:T(8,128)} fusion(bf16[2048,256]{1,0:T(8,128)(2,1)S(1)} %bitcast.18, bf16[2048,2048]{1,0:T(8,128)(2,1)} %all-gather.5.cloned.1.call-done), kind=kOutput, calls=%fused_computation.4 | convolution fusion | flops 2148007936 | bytes 11534336 | tf_op jit(solution)/shard_map/dot_general | solution.py:433
  (1 shorter events, 0.0 us)
Async XLA Ops:
  7.2 152.4 %all-gather.3.cloned.1.call-start = ((), (), s32[]{:S(2)}) async-start(), calls=%async_computation.1 | async-start | bytes 17825792 | tf_op jit(solution)/shard_map/all_gather | solution.py:331
  7.9 291.0 %all-gather.5.cloned.1.call-start = ((), (), s32[]{:S(2)}) async-start(), calls=%async_computation.2 | async-start | bytes 8912896 | tf_op jit(solution)/shard_map/all_gather | solution.py:409
  69.1 90.5 %copy-start = (bf16[128,4096]{1,0:T(8,128)(2,1)S(1)}, bf16[128,4096]{1,0:T(8,128)(2,1)}, u32[]{:S(2)}) copy-start(bf16[128,4096]{1,0:T(8,128)(2,1)} %get-tuple-element.28) | copy-start | bytes 3145732
  141.0 85.7 %copy-start.1 = (bf16[128,2048]{1,0:T(8,128)(2,1)S(1)}, bf16[128,2048]{1,0:T(8,128)(2,1)}, u32[]{:S(2)}) copy-start(bf16[128,2048]{1,0:T(8,128)(2,1)} %get-tuple-element.34) | copy-start | bytes 1572868
  233.0 32.0 %collective-permute-start = (bf16[128,2048]{1,0:T(8,128)(2,1)S(1)}, bf16[128,2048]{1,0:T(8,128)(2,1)S(1)}, u32[]{:S(2)}, u32[]{:S(2)}) collective-permute-start(bf16[128,2048]{1,0:T(8,128)(2,1)S(1)} %fusion.4), channel_id=1, source_target_pairs={{0,1},{1,0},{2,3},{3,2},{4,5},{5,4},{6,7},{7,6},{8,9},{9,8},{10,11... | collective-permute-start | bytes 1572872 | tf_op jit(solution)/shard_map/ppermute | solution.py:316
  234.5 29.9 %copy-start.2 = (f32[16,256]{1,0:T(8,128)S(1)}, f32[16,256]{1,0:T(8,128)}, u32[]{:S(2)}) copy-start(f32[16,256]{1,0:T(8,128)} %param.9) | copy-start | bytes 49156
Sparse Core Ops, SparseCore 0:
  10.2 149.3 all-gather.2
  226.8 72.0 all-gather.4
